TPU v7x, 128 devices: a whole 4x4x4 slice. The times are simulated.
128 devices in a mesh: dp: 16 (over y, z), tensor: 8 (over x, core).
Axes of the slice: x: 4, y: 4, z: 4, core: 2. Of those that a mesh axis runs over, the one named last changes fastest.
Arguments:
- activations: bfloat16 [16384, 8192], P('dp'), may hold values from -6 to 6
- output_grads: bfloat16 [2, 16384, 1024], P(None, 'dp', 'tensor'), may hold values from -0.1875 to 0.1875
- error_feedback: bfloat16 [2, 16, 8192, 1024], P(None, 'dp', None, 'tensor'), may hold values from -3 to 3
- warm_start: float32 [2, 1024, 8], P(None, 'tensor'), may hold values from -6 to 6
Outputs:
- decoded: bfloat16 [2, 8192, 1024], P(None, 'dp', 'tensor')
- new_error: bfloat16 [2, 16, 8192, 1024], P(None, 'dp', None, 'tensor')
All inputs are finite; a program needn't handle non-finite values.
Results may differ from a plain program's by a relative error of at most 0.0015.
Values sent between devices are 32-bit elements; how exact they have to be, the bound alone decides.
No kernel may reach another device: no remote copies, remote signals or barrier semaphores. Data moves between devices by JAX's collectives and lax.ppermute only.
A program may use at most 128 MiB of HBM per device.

v0:
```python
import jax
import jax.numpy as jnp
from jax import lax
from jax.sharding import PartitionSpec as P

ITERS = 2


HIGHEST = lax.Precision.HIGHEST


def lower_inverse(lower_factor):
    order = lower_factor.shape[-1]
    identity = jnp.eye(order, dtype=jnp.float32)
    inverse = jnp.zeros_like(lower_factor)
    for column in range(order):
        known = jnp.einsum("mj,mjk->mk", lower_factor[:, column, :], inverse, precision=HIGHEST)
        next_row = (identity[column][None, :] - known) / lower_factor[:, column, column][:, None]
        inverse = inverse.at[:, column, :].set(next_row)
    return inverse


def compress(segment, factor):
    basis = None
    for iteration in range(ITERS):
        partial_term = jnp.einsum("mdw,mwk->dmk", segment, factor, precision=HIGHEST)
        summed = lax.psum(partial_term, ("dp", "tensor"))
        gram_total = jnp.einsum("dmk,dml->mkl", summed, summed, precision=HIGHEST)
        inverse = lower_inverse(jnp.linalg.cholesky(gram_total))
        basis = jnp.einsum("dmk,mlk->dml", summed, inverse, precision=HIGHEST)
        right_term = jnp.einsum("mdw,dmk->mwk", segment, basis, precision=HIGHEST)
        factor = lax.psum(right_term, "dp")
    return (basis, factor)


def local(activations, output_grads, error_feedback, warm_start):
    replicas = lax.axis_size("dp")
    updates = jnp.einsum(
        "td,mtw->mdw", activations, output_grads, preferred_element_type=jnp.float32
    )
    updates = updates + error_feedback[:, 0].astype(jnp.float32)
    groups = ((0, 1), (1, 2))
    pieces = []
    for first, finish in groups:
        basis, factor = compress(updates[first:finish], warm_start[first:finish])
        pieces.append(jnp.einsum("dmk,mwk->mdw", basis, factor, precision=HIGHEST))
    mean_update = jnp.concatenate(pieces, axis=0) / replicas
    new_error = (updates - mean_update).astype(jnp.bfloat16)[:, None]
    row_count = mean_update.shape[1] // replicas
    own_rows = lax.dynamic_slice_in_dim(mean_update, lax.axis_index("dp") * row_count, row_count, 1)
    return (own_rows.astype(jnp.bfloat16), new_error)


def solution(mesh):
    placed = (
        P("dp", None),
        P(None, "dp", "tensor"),
        P(None, "dp", None, "tensor"),
        P(None, "tensor", None),
    )
    return jax.shard_map(
        local,
        mesh=mesh,
        in_specs=placed,
        out_specs=(P(None, "dp", "tensor"), P(None, "dp", None, "tensor")),
        check_vma=False,
    )
```

profile of v0, /device:TPU:0, one launch (start us, length us, event | category | flops | bytes accessed | tf_op | source)
XLA Modules:
  0.0 576.1 jit_solution(16998802388952987220)
XLA Ops:
  7.2 6.4 %copy.7 = bf16[2,1,8192,128]{2,3,0,1:T(8,128)(2,1)} copy(bf16[2,1,8192,128]{3,2,1,0:T(8,128)(2,1)} %param.71) | data formatting | bytes 8388608 | tf_op args[2]
  13.6 12.3 %fusion.5 = f32[2,8192,128]{1,2,0:T(8,128)S(1)} fusion(bf16[2,1024,128]{2,1,0:T(8,128)(2,1)S(1)} %copy-done, bf16[1024,8192]{1,0:T(8,128)(2,1)} %param.69, bf16[2,1,8192,128]{2,3,0,1:T(8,128)(2,1)} %copy.7), kind=kOutput, calls=%fused_computation.3 | convolution fusion | flops 4299161600 | bytes 29884416 | tf_op jit(solution)/shard_map/td,mtw->mdw/dot_general | solution.py:38
  25.9 3.5 fusion.11
  29.4 3.0 fusion.14
  32.4 147.3 %all-reduce.13.cloned.1.call-done = (f32[8192,8]{0,1:T(8,128)}, f32[8192,8]{0,1:T(8,128)}) async-done(((f32[8192,8]{0,1:T(8,128)}, f32[8192,8]{0,1:T(8,128)}), (f32[8192,8]{0,1:T(8,128)}, f32[8192,8]{0,1:T(8,128)})) %all-reduce.13.cloned.1.call-update) | async-done | bytes 524304 | tf_op jit(solution)/shard_map/psum | solution.py:27
  179.8 1.7 convolution_bitcast_fusion.11
  181.6 0.7 custom-call.6
  184.3 0.7 fusion.16
  185.0 0.8 fusion.17
  185.8 0.8 fusion.18
  186.6 0.7 fusion.19
  187.3 0.8 fusion.20
  188.1 0.8 fusion.21
  188.9 0.8 fusion.22
  189.7 0.8 fusion.23
  190.5 1.3 convolution_bitcast_fusion.7
  191.8 5.2 fusion.10
  197.0 1.7 convolution_bitcast_fusion.9
  198.8 0.7 custom-call.8
  201.5 0.7 fusion.34
  202.3 0.8 fusion.35
  203.0 0.7 fusion.36
  203.8 0.8 fusion.37
  204.5 0.7 fusion.38
  205.3 0.8 fusion.39
  206.0 0.8 fusion.40
  206.9 0.8 fusion.41
  207.8 1.3 convolution_bitcast_fusion.4
  209.2 5.2 fusion.13
  214.3 74.0 %all-reduce.7 = (f32[128,8]{1,0:T(8,128)S(1)}, f32[128,8]{1,0:T(8,128)S(1)}) all-reduce(f32[128,8]{1,0:T(8,128)S(1)} %fusion.13, f32[128,8]{1,0:T(8,128)S(1)} %fusion.10), channel_id=1, replica_groups=mesh['dp'=16,'tensor'=8] {'dp'}, use_global_device_ids=true, to_apply=%region_7.0 | all-reduce | flops 2048 | bytes 16384 | tf_op jit(solution)/shard_map/psum | solution.py:32
  288.3 5.0 convolution_bitcast_fusion.6
  293.3 5.0 convolution_bitcast_fusion.3
  298.3 140.0 %all-reduce.11.cloned.1.call-done = (f32[8192,8]{0,1:T(8,128)}, f32[8192,8]{0,1:T(8,128)}) async-done(((f32[8192,8]{0,1:T(8,128)}, f32[8192,8]{0,1:T(8,128)}), (f32[8192,8]{0,1:T(8,128)}, f32[8192,8]{0,1:T(8,128)})) %all-reduce.11.cloned.1.call-update) | async-done | bytes 524304 | tf_op jit(solution)/shard_map/psum | solution.py:27
  438.2 1.7 convolution_bitcast_fusion.10
  440.0 0.7 custom-call.7
  443.4 0.8 fusion.26
  444.2 0.8 fusion.27
  445.0 0.7 fusion.28
  445.8 0.8 fusion.29
  446.6 0.8 fusion.30
  447.4 0.8 fusion.31
  448.2 0.8 fusion.32
  449.0 1.3 convolution_bitcast_fusion.5
  450.3 5.2 fusion.9
  455.5 1.7 convolution_bitcast_fusion.8
  457.3 0.7 custom-call.9
  460.0 0.7 fusion.43
  460.7 0.8 fusion.44
  461.5 0.7 fusion.45
  462.2 0.8 fusion.46
  463.0 0.7 fusion.47
  463.7 0.8 fusion.48
  464.5 0.8 fusion.49
  465.3 0.8 fusion.50
  466.1 1.3 convolution_bitcast_fusion.2
  467.5 5.2 fusion.12
  472.6 74.2 %all-reduce.6 = (f32[128,8]{1,0:T(8,128)S(1)}, f32[128,8]{1,0:T(8,128)S(1)}) all-reduce(f32[128,8]{1,0:T(8,128)S(1)} %fusion.12, f32[128,8]{1,0:T(8,128)S(1)} %fusion.9), channel_id=1, replica_groups=mesh['dp'=16,'tensor'=8] {'dp'}, use_global_device_ids=true, to_apply=%region_9.0 | all-reduce | flops 2048 | bytes 16384 | tf_op jit(solution)/shard_map/psum | solution.py:32
  546.8 3.4 convolution_bitcast_fusion.1
  550.2 3.4 convolution_bitcast_fusion
  553.6 5.3 fusion.8
  559.0 2.2 maximum_multiply_fusion
  561.2 6.3 %copy.15 = bf16[2,1,8192,128]{3,2,1,0:T(8,128)(2,1)} copy(bf16[2,1,8192,128]{2,3,0,1:T(8,128)(2,1)} %fusion.8) | data formatting | bytes 8388608
  567.5 1.0 dynamic-slice_convert_fusion
  568.5 0.8 copy.14
  (68 shorter events, 10.0 us)
Async XLA Ops:
  7.2 6.4 %copy-start = (bf16[2,1024,128]{2,1,0:T(8,128)(2,1)S(1)}, bf16[2,1024,128]{2,1,0:T(8,128)(2,1)}, u32[]{:S(2)}) copy-start(bf16[2,1024,128]{2,1,0:T(8,128)(2,1)} %param.70) | copy-start | bytes 1572868
  7.2 172.6 %all-reduce.13.cloned.1.call-start = ((), (), s32[]{:S(2)}) async-start(), calls=%async_computation.1 | async-start | bytes 1048576 | tf_op jit(solution)/shard_map/psum | solution.py:27
  13.6 12.3 %copy-start.2 = (f32[2,128,8]{1,2,0:T(8,128)S(1)}, f32[2,128,8]{1,2,0:T(8,128)}, u32[]{:S(2)}) copy-start(f32[2,128,8]{1,2,0:T(8,128)} %param.72) | copy-start | bytes 24580
  25.9 3.5 copy-start.1
  32.4 405.9 %all-reduce.11.cloned.1.call-start = ((), (), s32[]{:S(2)}) async-start(), calls=%async_computation | async-start | bytes 1048576 | tf_op jit(solution)/shard_map/psum | solution.py:27
Sparse Core Ops, SparseCore 0:
  32.5 147.2 all-reduce.12
  298.4 139.7 all-reduce.10
where the time goes:
time: 577 us; the launch traced here: 576 us
  waiting for transfers between devices  287 us (50%)
  blocking collectives  148 us (26%)
  matrix products  92.2 us (16%)
  local copies, waits for them, and re-layouts  18.3 us (3%)
  other arithmetic  15.8 us (3%)
  between operations  14.3 us (2%)
    psum x2, waiting for transfers between devices, compress(): summed = lax.psum(partial_term, ('dp', 'tensor'))  287 us
    psum x2, blocking collectives, compress(): factor = lax.psum(right_term, 'dp')  148 us
    dot_general x32, matrix products, lower_inverse(): jnp.einsum('mj,mjk->mk', lower_factor[:, column, :], inverse, precision=H...  24 us
    dot_general x4, matrix products, compress(): right_term = jnp.einsum('mdw,dmk->mwk', segment, basis, precision=HIGHEST)  20.6 us
    dot_general x4, matrix products, compress(): jnp.einsum('mdw,mwk->dmk', segment, factor, precision=HIGHEST)  16.4 us
    unnamed x9, local copies, waits for them, and re-layouts  13.5 us
    dot_general x1, matrix products, local(): jnp.einsum('td,mtw->mdw', activations, output_grads, preferred_element_ty...  12.3 us
  transfers between devices with their start and end apart: 2, of which 2 were waited for; matrix products, arithmetic and copies ran while one was open for 0% of the time, Pallas kernels for 0%

commit v1 on v0

v1 whole, which is shorter than its diff:
```python
import functools

import jax
import jax.numpy as jnp
from jax import lax
from jax.experimental import pallas as pl
from jax.experimental.pallas import tpu as pltpu
from jax.sharding import PartitionSpec as P

RANK = 8
LANES = 128
F32, BF16 = jnp.float32, jnp.bfloat16
HIGHEST = lax.Precision.HIGHEST
EVERY = ("dp", "tensor")
NT = (((1,), (1,)), ((), ()))
TN = (((0,), (0,)), ((), ()))


def split(x):
    high = x.astype(BF16)
    return high, (x - high.astype(F32)).astype(BF16)


def dot(x, y, dims=(((1,), (0,)), ((), ()))):
    return lax.dot_general(x, y, dims, preferred_element_type=F32)


def block_diagonal(rows):
    zero = jnp.zeros_like(rows[0])
    top = jnp.concatenate([rows[0], zero], axis=1)
    bottom = jnp.concatenate([zero, rows[1]], axis=1)
    return jnp.concatenate([top, bottom], axis=0)


def left_terms(factor_rows, high, low):
    f_high, f_low = split(factor_rows)
    both = dot(jnp.concatenate([f_high, f_low], axis=0), high)
    return both[:16] + both[16:] + dot(f_high, low)


def store_tiles(out_ref, terms):
    for m in range(2):
        for b in range(terms.shape[1] // LANES):
            out_ref[m, b] = terms[m * RANK : (m + 1) * RANK, b * LANES : (b + 1) * LANES]


def rows_of(tiles_ref, m):
    return jnp.concatenate([tiles_ref[m, b] for b in range(tiles_ref.shape[1])], axis=1)


def updates_kernel(grads_ref, warm_ref, act_ref, error_ref, high_ref, low_ref, term_ref, grads_t):
    @pl.when(pl.program_id(0) == 0)
    def _():
        for m in range(2):
            grads_t[m * LANES : (m + 1) * LANES] = grads_ref[m].T

    errors = jnp.concatenate([error_ref[m, 0].T for m in range(2)], axis=0)
    updates = dot(grads_t[...], act_ref[...]) + errors.astype(F32)
    high, low = split(updates)
    high_ref[...] = high
    low_ref[...] = low
    warm = block_diagonal([warm_ref[m].T for m in range(2)])
    store_tiles(term_ref, left_terms(warm, high, low))


def make_updates(activations, output_grads, error_feedback, warm_start):
    tokens, d = activations.shape
    block = min(1024, d)
    wide = 2 * LANES
    return pl.pallas_call(
        updates_kernel,
        grid=(d // block,),
        in_specs=[
            pl.BlockSpec(output_grads.shape, lambda i: (0, 0, 0)),
            pl.BlockSpec(warm_start.shape, lambda i: (0, 0, 0)),
            pl.BlockSpec((tokens, block), lambda i: (0, i)),
            pl.BlockSpec((2, 1, block, LANES), lambda i: (0, 0, i, 0)),
        ],
        out_specs=[
            pl.BlockSpec((wide, block), lambda i: (0, i)),
            pl.BlockSpec((wide, block), lambda i: (0, i)),
            pl.BlockSpec((2, block // LANES, RANK, LANES), lambda i: (0, i, 0, 0)),
        ],
        out_shape=[
            jax.ShapeDtypeStruct((wide, d), BF16),
            jax.ShapeDtypeStruct((wide, d), BF16),
            jax.ShapeDtypeStruct((2, d // LANES, RANK, LANES), F32),
        ],
        scratch_shapes=[pltpu.VMEM((wide, tokens), BF16)],
        compiler_params=pltpu.CompilerParams(vmem_limit_bytes=28 << 20),
        name="updates",
    )(output_grads, warm_start, activations, error_feedback)


def inverse_of_factor(gram):
    row = lax.broadcasted_iota(jnp.int32, (RANK, 2 * RANK), 0)
    column = lax.broadcasted_iota(jnp.int32, (RANK, 2 * RANK), 1)
    table = jnp.concatenate([gram, jnp.zeros_like(gram)], axis=1)
    table = jnp.where(column == row + RANK, jnp.float32(1), table)
    for k in range(RANK):
        scale = 1.0 / jnp.sqrt(table[k : k + 1, k : k + 1])
        pivot = table[k : k + 1, :] * scale
        below = table - (table[:, k : k + 1] * scale) * pivot
        table = jnp.where(row > k, below, jnp.where(row == k, pivot, table))
    return table[:, RANK:]


def right_kernel(last, tiles_ref, high_ref, low_ref, out_ref):
    sums = [rows_of(tiles_ref, m) for m in range(2)]
    both = jnp.concatenate(sums, axis=0)
    s_high, s_low = split(both)
    pair = dot(jnp.concatenate([s_high, s_low], axis=0), high_ref[...], NT)
    right = pair[:16] + pair[16:] + dot(s_high, low_ref[...], NT)
    for m in range(2):
        gram = lax.dot_general(sums[m], sums[m], NT, precision=HIGHEST, preferred_element_type=F32)
        inverse = inverse_of_factor(gram)
        mine = right[m * RANK : (m + 1) * RANK, m * LANES : (m + 1) * LANES]
        factor = lax.dot_general(inverse, mine, (((1,), (0,)), ((), ())), precision=HIGHEST, preferred_element_type=F32)
        if last:
            factor = lax.dot_general(inverse, factor, TN, precision=HIGHEST, preferred_element_type=F32)
        for copy in range(out_ref.shape[0]):
            out_ref[copy, m] = factor


def right_terms(last, copies, tiles, high, low):
    return pl.pallas_call(
        functools.partial(right_kernel, last),
        out_shape=jax.ShapeDtypeStruct((copies, 2, RANK, LANES), F32),
        compiler_params=pltpu.CompilerParams(vmem_limit_bytes=28 << 20),
        name="right",
    )(tiles, high, low)


def total_rows(parts_ref):
    return [sum(parts_ref[r, m] for r in range(parts_ref.shape[0])) for m in range(2)]


def left_kernel(parts_ref, high_ref, low_ref, term_ref):
    factor = block_diagonal(total_rows(parts_ref))
    store_tiles(term_ref, left_terms(factor, high_ref[...], low_ref[...]))


def left_call(parts, high, low):
    wide, d = high.shape
    block = min(2048, d)
    return pl.pallas_call(
        left_kernel,
        grid=(d // block,),
        in_specs=[
            pl.BlockSpec(parts.shape, lambda i: (0, 0, 0, 0)),
            pl.BlockSpec((wide, block), lambda i: (0, i)),
            pl.BlockSpec((wide, block), lambda i: (0, i)),
        ],
        out_specs=pl.BlockSpec((2, block // LANES, RANK, LANES), lambda i: (0, i, 0, 0)),
        out_shape=jax.ShapeDtypeStruct((2, d // LANES, RANK, LANES), F32),
        compiler_params=pltpu.CompilerParams(vmem_limit_bytes=28 << 20),
        name="left",
    )(parts, high, low)


def spread_kernel(parts_ref, out_ref):
    total = parts_ref[0]
    for r in range(1, parts_ref.shape[0]):
        total = total + parts_ref[r]
    for r in range(parts_ref.shape[0]):
        out_ref[r] = total


def spread_sum(parts):
    return pl.pallas_call(
        spread_kernel,
        out_shape=jax.ShapeDtypeStruct(parts.shape, F32),
        compiler_params=pltpu.CompilerParams(vmem_limit_bytes=8 << 20),
        name="spread",
    )(parts)


def sum_everywhere(tiles):
    shape = tiles.shape
    flat = tiles.reshape((shape[0] * shape[1],) + shape[2:])
    mine = lax.all_to_all(flat, EVERY, 0, 0)
    return lax.all_to_all(spread_sum(mine), EVERY, 0, 0).reshape(shape)


def mean_columns(weights, tiles):
    w_high, w_low = split(weights)
    t_high, t_low = split(tiles)
    left = jnp.concatenate([w_high, w_high, w_low], axis=0)
    right = jnp.concatenate([t_high, t_low, t_high], axis=0)
    return dot(left, right, TN)


def final_kernel(replicas, own_ref, parts_ref, all_tiles_ref, tiles_ref, high_ref, low_ref, decoded_ref, error_ref):
    weights = [w / replicas for w in total_rows(parts_ref)]

    @pl.when(pl.program_id(0) == 0)
    def _():
        own = own_ref[0]
        count = decoded_ref.shape[1] // LANES
        for m in range(2):
            tiles = jnp.concatenate([all_tiles_ref[m, own * count + b] for b in range(count)], axis=1)
            decoded_ref[m] = mean_columns(weights[m], tiles).T.astype(BF16)

    for m in range(2):
        part = pl.ds(m * LANES, LANES)
        updates = high_ref[part, :].astype(F32) + low_ref[part, :].astype(F32)
        rest = updates - mean_columns(weights[m], rows_of(tiles_ref, m))
        error_ref[m, 0] = rest.astype(BF16).T


def final_call(own, replicas, parts, tiles, high, low):
    wide, d = high.shape
    block = min(1024, d)
    return pl.pallas_call(
        functools.partial(final_kernel, replicas),
        grid_spec=pltpu.PrefetchScalarGridSpec(
            num_scalar_prefetch=1,
            grid=(d // block,),
            in_specs=[
                pl.BlockSpec(parts.shape, lambda i, own: (0, 0, 0, 0)),
                pl.BlockSpec(tiles.shape, lambda i, own: (0, 0, 0, 0)),
                pl.BlockSpec((2, block // LANES, RANK, LANES), lambda i, own: (0, i, 0, 0)),
                pl.BlockSpec((wide, block), lambda i, own: (0, i)),
                pl.BlockSpec((wide, block), lambda i, own: (0, i)),
            ],
            out_specs=[
                pl.BlockSpec((2, d // replicas, LANES), lambda i, own: (0, 0, 0)),
                pl.BlockSpec((2, 1, block, LANES), lambda i, own: (0, 0, i, 0)),
            ],
        ),
        out_shape=[
            jax.ShapeDtypeStruct((2, d // replicas, LANES), BF16),
            jax.ShapeDtypeStruct((2, 1, d, LANES), BF16),
        ],
        compiler_params=pltpu.CompilerParams(vmem_limit_bytes=28 << 20),
        name="final",
    )(own, parts, tiles, tiles, high, low)


def local(activations, output_grads, error_feedback, warm_start):
    replicas = lax.axis_size("dp")
    high, low, term = make_updates(activations, output_grads, error_feedback, warm_start)
    summed = sum_everywhere(term)
    parts = lax.all_to_all(right_terms(False, replicas, summed, high, low), "dp", 0, 0)
    summed = sum_everywhere(left_call(parts, high, low))
    parts = lax.all_to_all(right_terms(True, replicas, summed, high, low), "dp", 0, 0)
    own = lax.axis_index("dp").reshape(1)
    return tuple(final_call(own, replicas, parts, summed, high, low))


def solution(mesh):
    placed = (
        P("dp", None),
        P(None, "dp", "tensor"),
        P(None, "dp", None, "tensor"),
        P(None, "tensor", None),
    )
    return jax.shard_map(
        local,
        mesh=mesh,
        in_specs=placed,
        out_specs=(P(None, "dp", "tensor"), P(None, "dp", None, "tensor")),
        check_vma=False,
    )
```

time: 577 us -> 144 us (0.25)
  waiting for transfers between devices: 287 us -> 7.77 us
  matrix products: 92.2 us -> 0 us
  blocking collectives: 148 us -> 89.9 us
  Pallas kernels: 0 us -> 32.7 us
  other arithmetic: 15.8 us -> 0 us
  between operations: 14.3 us -> 0.71 us
  local copies, waits for them, and re-layouts: 18.3 us -> 8.43 us
    psum x2 -> x0, waiting for transfers between devices: 287 us -> none  [compress(): summed = lax.psum(partial_term, ('dp', 'tensor'))]
    psum x2 -> x0, blocking collectives: 148 us -> none  [compress(): factor = lax.psum(right_term, 'dp')]
    dot_general x51 -> x0, matrix products: 92.2 us -> none  [the longest x32 24 us: lower_inverse(): jnp.einsum('mj,mjk->mk', lower_factor[:, column, :], inverse, precision=H...]
    all_to_all x0 -> x5, blocking collectives: none -> 89.9 us  [the longest x2 43.3 us: sum_everywhere(): mine = lax.all_to_all(flat, EVERY, 0, 0)]
    pallas_call x0 -> x7, Pallas kernels: none -> 32.7 us  [the longest x1 12.1 us: make_updates(): pl.pallas_call(updates_kernel, grid=(d // block,), in_specs=[pl.BlockSpec...]
    all_to_all x0 -> x1, waiting for transfers between devices: none -> 7.77 us  [local(): lax.all_to_all(right_terms(True, replicas, summed, high, low), 'dp', 0, 0)]
    unnamed x9 -> x13, local copies, waits for them, and re-layouts: 13.5 us -> 8.43 us
  transfers between devices with their start and end apart: 2 -> 1, of which waited for: 2 -> 1; matrix products, arithmetic and copies ran while one was open for 0% -> 0% of each run, Pallas kernels for 0% -> 0%
where the time goes in v1:
time: 144 us; the launch traced here: 143 us
  blocking collectives  89.9 us (62%)
  Pallas kernels  32.7 us (23%)
  local copies, waits for them, and re-layouts  8.43 us (6%)
  waiting for transfers between devices  7.77 us (5%)
  starting transfers between devices  3.51 us (2%)
    all_to_all x2, blocking collectives, sum_everywhere(): mine = lax.all_to_all(flat, EVERY, 0, 0)  43.3 us
    all_to_all x2, blocking collectives, sum_everywhere(): return lax.all_to_all(spread_sum(mine), EVERY, 0, 0).reshape(shape)  36.1 us
    pallas_call x1, Pallas kernels, make_updates(): pl.pallas_call(updates_kernel, grid=(d // block,), in_specs=[pl.BlockSpec...  12.1 us
    pallas_call x2, Pallas kernels, right_terms(): pl.pallas_call(functools.partial(right_kernel, last), out_shape=jax.Shape...  12 us
    all_to_all x1, blocking collectives, local(): lax.all_to_all(right_terms(False, replicas, summed, high, low), 'dp', 0, 0)  10.5 us
    unnamed x13, local copies, waits for them, and re-layouts  8.43 us
    all_to_all x1, waiting for transfers between devices, local(): lax.all_to_all(right_terms(True, replicas, summed, high, low), 'dp', 0, 0)  7.77 us
    pallas_call x1, Pallas kernels, final_call(): pl.pallas_call(functools.partial(final_kernel, replicas), grid_spec=pltpu...  5.97 us
  transfers between devices with their start and end apart: 1, of which 1 were waited for; matrix products, arithmetic and copies ran while one was open for 0% of the time, Pallas kernels for 0%

profile of v1, /device:TPU:0, one launch (start us, length us, event | category | flops | bytes accessed | tf_op | source)
XLA Modules:
  0.0 143.0 jit_solution(13049322656634814470)
XLA Ops:
  0.6 0.8 copy.6.warm_ref
  1.5 0.0 copy-start.4
  1.5 2.2 %copy-done.4 = bf16[2,1,8192,128]{3,2,1,0:T(8,128)(2,1)S(1)} copy-done((bf16[2,1,8192,128]{3,2,1,0:T(8,128)(2,1)S(1)}, bf16[2,1,8192,128]{3,2,1,0:T(8,128)(2,1)}, u32[]{:S(2)}) %copy-start.4) | copy-done | bytes 4194328
  3.6 0.0 copy-start.5
  3.7 1.0 copy-done.5
  4.7 12.1 %updates.1 = (bf16[256,8192]{1,0:T(8,128)(2,1)S(1)}, bf16[256,8192]{1,0:T(8,128)(2,1)S(1)}, f32[2,64,8,128]{3,2,1,0:T(8,128)S(1)}) custom-call(bf16[2,1024,128]{2,1,0:T(8,128)(2,1)S(1)} %copy-done.5, f32[2,128,8]{2,1,0:T(8,128)S(1)} %copy.6.warm_ref, bf16[1024,8192]{1,0:T(8,128)(2,1)} %act_ref.1, bf16[2,1,8192,128]{3,2,1,0:T(8,128)(2,1)S(1)} %copy-done.4), custom_call_target="tpu_custom_call" | custom-call | tf_op jit(solution)/shard_map/updates/pallas_call | solution.py:70
  16.8 0.0 copy-start
  16.9 0.0 copy-start.2
  16.9 24.5 %all_to_all.30.parts_ref = f32[128,8,128]{2,1,0:T(8,128)S(1)} all-to-all(f32[128,8,128]{2,1,0:T(8,128)S(1)} %bitcast.10), channel_id=1, replica_groups=mesh['dp'=16,'tensor'=8] {'dp','tensor'}, dimensions={0} | all-to-all | bytes 1048576 | tf_op jit(solution)/shard_map/all_to_all | solution.py:181
  41.4 0.2 spread.2
  41.5 18.0 %all_to_all.31 = f32[128,8,128]{2,1,0:T(8,128)S(1)} all-to-all(f32[128,8,128]{2,1,0:T(8,128)S(1)} %spread.2), channel_id=1, replica_groups=mesh['dp'=16,'tensor'=8] {'dp','tensor'}, dimensions={0} | all-to-all | bytes 1048576 | tf_op jit(solution)/shard_map/all_to_all | solution.py:182
  59.6 5.5 %right.2 = f32[16,2,8,128]{3,2,1,0:T(8,128)S(1)} custom-call(f32[2,64,8,128]{3,2,1,0:T(8,128)S(1)} %bitcast.8, bf16[256,8192]{1,0:T(8,128)(2,1)S(1)} %get-tuple-element.6.high_ref, bf16[256,8192]{1,0:T(8,128)(2,1)S(1)} %get-tuple-element.7.low_ref), custom_call_target="tpu_custom_call" | custom-call | tf_op jit(solution)/shard_map/right/pallas_call | solution.py:126
  65.1 10.5 %all_to_all.32.parts_ref = f32[16,2,8,128]{3,2,1,0:T(8,128)S(1)} all-to-all(f32[16,2,8,128]{3,2,1,0:T(8,128)S(1)} %right.2), channel_id=1, replica_groups=mesh['dp'=16,'tensor'=8] {'dp'}, dimensions={0} | all-to-all | bytes 262144 | tf_op jit(solution)/shard_map/all_to_all | solution.py:244
  75.6 2.3 %left.1 = f32[2,64,8,128]{3,2,1,0:T(8,128)S(1)} custom-call(f32[16,2,8,128]{3,2,1,0:T(8,128)S(1)} %all_to_all.32.parts_ref, bf16[256,8192]{1,0:T(8,128)(2,1)S(1)} %get-tuple-element.6.high_ref, bf16[256,8192]{1,0:T(8,128)(2,1)S(1)} %get-tuple-element.7.low_ref), custom_call_target="tpu_custom_call" | custom-call | tf_op jit(solution)/shard_map/left/pallas_call | solution.py:146
  77.9 18.8 %all_to_all.33.parts_ref = f32[128,8,128]{2,1,0:T(8,128)S(1)} all-to-all(f32[128,8,128]{2,1,0:T(8,128)S(1)} %bitcast.9), channel_id=1, replica_groups=mesh['dp'=16,'tensor'=8] {'dp','tensor'}, dimensions={0} | all-to-all | bytes 1048576 | tf_op jit(solution)/shard_map/all_to_all | solution.py:181
  96.7 0.2 spread.3
  96.8 18.0 %all_to_all.34 = f32[128,8,128]{2,1,0:T(8,128)S(1)} all-to-all(f32[128,8,128]{2,1,0:T(8,128)S(1)} %spread.3), channel_id=1, replica_groups=mesh['dp'=16,'tensor'=8] {'dp','tensor'}, dimensions={0} | all-to-all | bytes 1048576 | tf_op jit(solution)/shard_map/all_to_all | solution.py:182
  114.9 0.0 copy-done
  114.9 0.0 copy-done.2
  114.9 6.5 %right.3 = f32[16,2,8,128]{3,2,1,0:T(8,128)} custom-call(f32[2,64,8,128]{3,2,1,0:T(8,128)S(1)} %bitcast.5, bf16[256,8192]{1,0:T(8,128)(2,1)S(1)} %get-tuple-element.6.high_ref, bf16[256,8192]{1,0:T(8,128)(2,1)S(1)} %get-tuple-element.7.low_ref), custom_call_target="tpu_custom_call" | custom-call | tf_op jit(solution)/shard_map/right/pallas_call | solution.py:126
  121.3 3.5 %all-to-all-start.5 = ((f32[16,2,8,128]{3,2,1,0:T(8,128)}), f32[16,2,8,128]{3,2,1,0:T(8,128)S(1)}, u32[]{:S(2)}, u32[]{:S(2)}) async-start(f32[16,2,8,128]{3,2,1,0:T(8,128)} %right.3), calls=%async_computation.5 | async-start | bytes 262144 | tf_op jit(solution)/shard_map/all_to_all | solution.py:246
  124.9 7.8 %all-to-all-done.5.parts_ref = f32[16,2,8,128]{3,2,1,0:T(8,128)S(1)} async-done(((f32[16,2,8,128]{3,2,1,0:T(8,128)}), f32[16,2,8,128]{3,2,1,0:T(8,128)S(1)}, u32[]{:S(2)}, u32[]{:S(2)}) %all-to-all-start.5) | async-done | bytes 131104 | tf_op jit(solution)/shard_map/all_to_all | solution.py:246
  132.6 0.0 copy-start.1
  132.7 2.2 %copy-done.1 = bf16[256,8192]{1,0:T(8,128)(2,1)S(1)} copy-done((bf16[256,8192]{1,0:T(8,128)(2,1)S(1)}, bf16[256,8192]{1,0:T(8,128)(2,1)}, u32[]{:S(2)}) %copy-start.1) | copy-done | bytes 4194328
  134.8 0.0 copy-start.3
  134.8 2.2 %copy-done.3 = bf16[256,8192]{1,0:T(8,128)(2,1)S(1)} copy-done((bf16[256,8192]{1,0:T(8,128)(2,1)S(1)}, bf16[256,8192]{1,0:T(8,128)(2,1)}, u32[]{:S(2)}) %copy-start.3) | copy-done | bytes 4194328
  137.0 6.0 %final.1 = (bf16[2,512,128]{2,1,0:T(8,128)(2,1)}, bf16[2,1,8192,128]{3,2,1,0:T(8,128)(2,1)}) custom-call(s32[1]{0:T(128)} %bitcast.own_ref, f32[16,2,8,128]{3,2,1,0:T(8,128)S(1)} %all-to-all-done.5.parts_ref, f32[2,64,8,128]{3,2,1,0:T(8,128)S(1)} %bitcast.6, f32[2,64,8,128]{3,2,1,0:T(8,128)S(1)} %bitcast.7, bf16[256,8192]{1,0:T(8,128)(2,1)S(1)} %copy-done.1, ...), custom_call_target="tpu_custom_call" | custom-call | tf_op jit(solution)/shard_map/final/pallas_call | solution.py:214
Async XLA Ops:
  1.5 2.2 %copy-start.4 = (bf16[2,1,8192,128]{3,2,1,0:T(8,128)(2,1)S(1)}, bf16[2,1,8192,128]{3,2,1,0:T(8,128)(2,1)}, u32[]{:S(2)}) copy-start(bf16[2,1,8192,128]{3,2,1,0:T(8,128)(2,1)} %error_ref.1) | copy-start | bytes 12582916
  3.6 1.0 copy-start.5
  16.8 98.0 %copy-start = (bf16[256,8192]{1,0:T(8,128)(2,1)}, bf16[256,8192]{1,0:T(8,128)(2,1)S(1)}, u32[]{:S(2)}) copy-start(bf16[256,8192]{1,0:T(8,128)(2,1)S(1)} %get-tuple-element.6.high_ref) | copy-start | bytes 12582916
  16.9 98.0 %copy-start.2 = (bf16[256,8192]{1,0:T(8,128)(2,1)}, bf16[256,8192]{1,0:T(8,128)(2,1)S(1)}, u32[]{:S(2)}) copy-start(bf16[256,8192]{1,0:T(8,128)(2,1)S(1)} %get-tuple-element.7.low_ref) | copy-start | bytes 12582916
  121.3 11.3 %all-to-all-start.5 = ((f32[16,2,8,128]{3,2,1,0:T(8,128)}), f32[16,2,8,128]{3,2,1,0:T(8,128)S(1)}, u32[]{:S(2)}, u32[]{:S(2)}) async-start(f32[16,2,8,128]{3,2,1,0:T(8,128)} %right.3), calls=%async_computation.5 | async-start | bytes 262144 | tf_op jit(solution)/shard_map/all_to_all | solution.py:246
  132.6 2.2 %copy-start.1 = (bf16[256,8192]{1,0:T(8,128)(2,1)S(1)}, bf16[256,8192]{1,0:T(8,128)(2,1)}, u32[]{:S(2)}) copy-start(bf16[256,8192]{1,0:T(8,128)(2,1)} %copy-done) | copy-start | bytes 12582916
  134.8 2.2 %copy-start.3 = (bf16[256,8192]{1,0:T(8,128)(2,1)S(1)}, bf16[256,8192]{1,0:T(8,128)(2,1)}, u32[]{:S(2)}) copy-start(bf16[256,8192]{1,0:T(8,128)(2,1)} %copy-done.2) | copy-start | bytes 12582916

commit v2 on v0

v2 whole, which is shorter than its diff:
```python
import functools

import jax
import jax.numpy as jnp
from jax import lax
from jax.experimental import pallas as pl
from jax.experimental.pallas import tpu as pltpu
from jax.sharding import PartitionSpec as P

RANK = 8
CHUNK = 1024
LANES = 128
F32, BF16 = jnp.float32, jnp.bfloat16
HIGHEST = lax.Precision.HIGHEST
EVERY = ("dp", "tensor")
NN = (((1,), (0,)), ((), ()))
NT = (((1,), (1,)), ((), ()))
TN = (((0,), (0,)), ((), ()))
WHOLE = pl.BlockSpec(memory_space=pltpu.VMEM)
in_vmem = functools.partial(pltpu.with_memory_space_constraint, memory_space=pltpu.VMEM)
in_hbm = functools.partial(pltpu.with_memory_space_constraint, memory_space=pltpu.HBM)


def params(mebibytes):
    return pltpu.CompilerParams(vmem_limit_bytes=mebibytes << 20)


def split(x):
    high = x.astype(BF16)
    return high, (x - high.astype(F32)).astype(BF16)


def dot(x, y, dims=NN):
    return lax.dot_general(x, y, dims, preferred_element_type=F32)


def exact_dot(x, y, dims=NN):
    return lax.dot_general(x, y, dims, precision=HIGHEST, preferred_element_type=F32)


def two_terms(x):
    return jnp.concatenate(split(x), axis=0)


def folded(pair):
    half = pair.shape[0] // 2
    return pair[:half] + pair[half:]


def block_diagonal(rows):
    zero = jnp.zeros_like(rows[0])
    top = jnp.concatenate([rows[0], zero], axis=1)
    bottom = jnp.concatenate([zero, rows[1]], axis=1)
    return jnp.concatenate([top, bottom], axis=0)


def store_tiles(out_ref, terms, first=0):
    for m in range(2):
        for b in range(terms.shape[1] // LANES):
            out_ref[m, first + b] = terms[m * RANK : (m + 1) * RANK, b * LANES : (b + 1) * LANES]


def rows_of(tiles_ref, m, first=0, count=None):
    count = tiles_ref.shape[1] if count is None else count
    return jnp.concatenate([tiles_ref[m, first + b] for b in range(count)], axis=1)


def updates_kernel(chunk, act_ref, grads_ref, error_ref, warm_ref, high_ref, low_ref, term_ref, act, grads, errors, sems):
    tokens, d = act.shape
    parts = [pl.ds(first, chunk) for first in range(0, d, chunk)]
    grads_copy = pltpu.make_async_copy(grads_ref, grads, sems.at[0])
    grads_copy.start()
    copies = []
    for i, part in enumerate(parts):
        copies.append(
            [
                pltpu.make_async_copy(error_ref.at[:, :, part], errors.at[:, :, part], sems.at[2 * i + 1]),
                pltpu.make_async_copy(act_ref.at[:, part], act.at[:, part], sems.at[2 * i + 2]),
            ]
        )
        for copy in copies[-1]:
            copy.start()
    warm = [two_terms(warm_ref[m]) for m in range(2)]
    identity = jnp.where(
        lax.broadcasted_iota(jnp.int32, (LANES, LANES), 0) == lax.broadcasted_iota(jnp.int32, (LANES, LANES), 1), 1.0, 0.0
    ).astype(BF16)
    turn = [jnp.concatenate([identity, warm[m]], axis=0) for m in range(2)]
    grads_copy.wait()
    taken = two_terms(jnp.concatenate([folded(dot(warm[m], grads[m], NT)) for m in range(2)], axis=0))
    weights = jnp.concatenate([grads[0].T, grads[1].T, taken], axis=0)
    wide = 2 * LANES
    for i, part in enumerate(parts):
        for copy in copies[i]:
            copy.wait()
        turned = [dot(turn[m], errors[m, 0, part], NT) for m in range(2)]
        products = dot(weights, act[:, part])
        high, low = split(products[:wide] + jnp.concatenate([t[:LANES] for t in turned], axis=0))
        high_ref[:, part] = high
        low_ref[:, part] = low
        terms = jnp.concatenate([folded(t[LANES:]) for t in turned], axis=0)
        store_tiles(term_ref, folded(products[wide:]) + terms, i * chunk // LANES)


def make_updates(activations, output_grads, error_feedback, warm_rows):
    tokens, d = activations.shape
    chunk = min(CHUNK, d)
    wide = 2 * LANES
    loaded = (activations, output_grads, error_feedback)
    return pl.pallas_call(
        functools.partial(updates_kernel, chunk),
        in_specs=[pl.BlockSpec(memory_space=pl.ANY)] * 3 + [WHOLE],
        out_specs=[WHOLE] * 3,
        out_shape=[pltpu.VMEM((wide, d), BF16)] * 2 + [jax.ShapeDtypeStruct((2, d // LANES, RANK, LANES), F32)],
        scratch_shapes=[pltpu.VMEM(x.shape, x.dtype) for x in loaded] + [pltpu.SemaphoreType.DMA((1 + 2 * (d // chunk),))],
        compiler_params=params(32),
        name="updates",
    )(*map(in_hbm, loaded), warm_rows)


def inverse_of_factor(gram):
    row = lax.broadcasted_iota(jnp.int32, (RANK, 2 * RANK), 0)
    column = lax.broadcasted_iota(jnp.int32, (RANK, 2 * RANK), 1)
    table = jnp.concatenate([gram, jnp.zeros_like(gram)], axis=1)
    table = jnp.where(column == row + RANK, jnp.float32(1), table)
    pivots = jnp.zeros((RANK, 2 * RANK), F32)
    for k in range(RANK):
        along = jnp.broadcast_to(table[:, k : k + 1], table.shape)
        pivot = jnp.broadcast_to(along[k : k + 1, :], table.shape)
        pivots = jnp.where(row == k, pivot, pivots)
        table = jnp.where(row > k, table - (along / pivot) * table[k : k + 1, :], table)
    return (table * (1.0 / jnp.sqrt(pivots)))[:, RANK:]


def right_kernel(last, tiles_ref, high_ref, low_ref, out_ref):
    sums = [rows_of(tiles_ref, m) for m in range(2)]
    grams = [exact_dot(rows, rows, NT) for rows in sums]
    s_high, s_low = split(jnp.concatenate(sums, axis=0))
    pair = dot(jnp.concatenate([s_high, s_low], axis=0), high_ref[...], NT)
    right = folded(pair) + dot(s_high, low_ref[...], NT)
    inverses = [inverse_of_factor(gram) for gram in grams]
    for m in range(2):
        norm = exact_dot(inverses[m], inverses[m], TN) if last else inverses[m]
        mine = exact_dot(norm, right[m * RANK : (m + 1) * RANK, m * LANES : (m + 1) * LANES])
        for copy in range(out_ref.shape[0]):
            out_ref[copy, m] = mine


def right_terms(last, copies, tiles, high, low):
    return pl.pallas_call(
        functools.partial(right_kernel, last),
        in_specs=[WHOLE] * 3,
        out_specs=WHOLE,
        out_shape=jax.ShapeDtypeStruct((copies, 2, RANK, LANES), F32),
        compiler_params=params(24),
        name="right",
    )(tiles, in_vmem(high), in_vmem(low))


def totals(parts_ref):
    return [sum(parts_ref[r, m] for r in range(parts_ref.shape[0])) for m in range(2)]


def left_kernel(parts_ref, high_ref, low_ref, term_ref):
    f_high, f_low = split(block_diagonal(totals(parts_ref)))
    both = jnp.concatenate([f_high, f_low], axis=0)
    step = min(2048, high_ref.shape[1])
    for first in range(0, high_ref.shape[1], step):
        part = pl.ds(first, step)
        terms = folded(dot(both, high_ref[:, part])) + dot(f_high, low_ref[:, part])
        store_tiles(term_ref, terms, first // LANES)


def left_terms(parts, high, low):
    return pl.pallas_call(
        left_kernel,
        in_specs=[WHOLE] * 3,
        out_specs=WHOLE,
        out_shape=jax.ShapeDtypeStruct((2, high.shape[1] // LANES, RANK, LANES), F32),
        compiler_params=params(24),
        name="left",
    )(parts, in_vmem(high), in_vmem(low))


def spread_kernel(parts_ref, out_ref):
    total = parts_ref[0]
    for r in range(1, parts_ref.shape[0]):
        total = total + parts_ref[r]
    for r in range(parts_ref.shape[0]):
        out_ref[r] = total


def spread_sum(parts):
    return pl.pallas_call(
        spread_kernel,
        in_specs=[WHOLE],
        out_specs=WHOLE,
        out_shape=jax.ShapeDtypeStruct(parts.shape, F32),
        compiler_params=params(8),
        name="spread",
    )(parts)


def scatter_sum(tiles):
    return lax.all_to_all(tiles.reshape((-1,) + tiles.shape[2:]), EVERY, 0, 0)


def gather_sum(parts, shape):
    return lax.all_to_all(spread_sum(parts), EVERY, 0, 0).reshape(shape)


def mean_columns(weights, tiles):
    w_high, w_low = split(weights)
    t_high, t_low = split(tiles)
    left = jnp.concatenate([w_high, w_high, w_low], axis=0)
    right = jnp.concatenate([t_high, t_low, t_high], axis=0)
    return dot(left, right, TN)


def final_kernel(replicas, block, parts_ref, tiles_ref, high_ref, low_ref, decoded_ref, error_ref, held, sems):
    weights = [w / replicas for w in totals(parts_ref)]
    copies = []
    for i in range(high_ref.shape[1] // block):
        columns = pl.ds(i * block, block)
        for m in range(2):
            part = pl.ds(m * LANES, LANES)
            updates = high_ref[part, columns].astype(F32) + low_ref[part, columns].astype(F32)
            tiles = rows_of(tiles_ref, m, i * block // LANES, block // LANES)
            held[m, 0, columns] = (updates - mean_columns(weights[m], tiles)).astype(BF16).T
        copy = pltpu.make_async_copy(held.at[:, :, columns], error_ref.at[:, :, columns], sems.at[i])
        copy.start()
        copies.append(copy)
    count = decoded_ref.shape[1] // LANES
    for m in range(2):
        tiles = rows_of(tiles_ref, m, lax.axis_index("dp") * count, count)
        decoded_ref[m] = mean_columns(weights[m], tiles).T.astype(BF16)
    for copy in copies:
        copy.wait()


def final_outputs(replicas, parts, tiles, high, low):
    d = high.shape[1]
    block = min(1024, d)
    return pl.pallas_call(
        functools.partial(final_kernel, replicas, block),
        in_specs=[WHOLE] * 4,
        out_specs=[WHOLE, pl.BlockSpec(memory_space=pl.ANY)],
        out_shape=[
            jax.ShapeDtypeStruct((2, d // replicas, LANES), BF16),
            jax.ShapeDtypeStruct((2, 1, d, LANES), BF16),
        ],
        scratch_shapes=[pltpu.VMEM((2, 1, d, LANES), BF16), pltpu.SemaphoreType.DMA((d // block,))],
        compiler_params=params(24),
        name="final",
    )(parts, tiles, in_vmem(high), in_vmem(low))


def local(activations, output_grads, error_feedback, warm_start):
    replicas = lax.axis_size("dp")
    high, low, term = make_updates(activations, output_grads, error_feedback, jnp.swapaxes(warm_start, 1, 2))
    summed = gather_sum(scatter_sum(term), term.shape)
    parts = lax.all_to_all(right_terms(False, replicas, summed, high, low), "dp", 0, 0)
    summed = gather_sum(scatter_sum(left_terms(parts, high, low)), term.shape)
    parts = lax.all_to_all(right_terms(True, replicas, summed, high, low), "dp", 0, 0)
    return tuple(final_outputs(replicas, parts, summed, high, low))


def solution(mesh):
    placed = (
        P("dp", None),
        P(None, "dp", "tensor"),
        P(None, "dp", None, "tensor"),
        P(None, "tensor", None),
    )
    return jax.shard_map(
        local,
        mesh=mesh,
        in_specs=placed,
        out_specs=(P(None, "dp", "tensor"), P(None, "dp", None, "tensor")),
        check_vma=False,
    )
```

time: 577 us -> 125 us (0.22)
  waiting for transfers between devices: 287 us -> 0 us
  matrix products: 92.2 us -> 0 us
  blocking collectives: 148 us -> 100 us
  Pallas kernels: 0 us -> 22.4 us
  local copies, waits for them, and re-layouts: 18.3 us -> 0.69 us
  other arithmetic: 15.8 us -> 0 us
  between operations: 14.3 us -> 0.82 us
    psum x2 -> x0, waiting for transfers between devices: 287 us -> none  [compress(): summed = lax.psum(partial_term, ('dp', 'tensor'))]
    psum x2 -> x0, blocking collectives: 148 us -> none  [compress(): factor = lax.psum(right_term, 'dp')]
    all_to_all x0 -> x6, blocking collectives: none -> 100 us  [the longest x2 43.2 us: scatter_sum(): return lax.all_to_all(tiles.reshape((-1,) + tiles.shape[2:]), EVERY, 0, 0)]
    dot_general x51 -> x0, matrix products: 92.2 us -> none  [the longest x32 24 us: lower_inverse(): jnp.einsum('mj,mjk->mk', lower_factor[:, column, :], inverse, precision=H...]
    pallas_call x0 -> x7, Pallas kernels: none -> 22.4 us  [the longest x1 9.75 us: make_updates(): pl.pallas_call(functools.partial(updates_kernel, chunk), in_specs=[pl.Blo...]
    unnamed x9 -> x2, local copies, waits for them, and re-layouts: 13.5 us -> 0.69 us
  transfers between devices with their start and end apart: 2 -> 0, of which waited for: 2 -> 0; matrix products, arithmetic and copies ran while one was open for 0% -> 0% of each run, Pallas kernels for 0% -> 0%
where the time goes in v2:
time: 125 us; the launch traced here: 124 us
  blocking collectives  100 us (80%)
  Pallas kernels  22.4 us (18%)
    all_to_all x2, blocking collectives, scatter_sum(): return lax.all_to_all(tiles.reshape((-1,) + tiles.shape[2:]), EVERY, 0, 0)  43.2 us
    all_to_all x2, blocking collectives, gather_sum(): return lax.all_to_all(spread_sum(parts), EVERY, 0, 0).reshape(shape)  36.1 us
    all_to_all x1, blocking collectives, local(): lax.all_to_all(right_terms(False, replicas, summed, high, low), 'dp', 0, 0)  10.5 us
    all_to_all x1, blocking collectives, local(): lax.all_to_all(right_terms(True, replicas, summed, high, low), 'dp', 0, 0)  10.5 us
    pallas_call x1, Pallas kernels, make_updates(): pl.pallas_call(functools.partial(updates_kernel, chunk), in_specs=[pl.Blo...  9.75 us
    pallas_call x2, Pallas kernels, right_terms(): pl.pallas_call(functools.partial(right_kernel, last), in_specs=[WHOLE] *...  7.18 us
    pallas_call x1, Pallas kernels, final_outputs(): pl.pallas_call(functools.partial(final_kernel, replicas, block), in_specs...  3.77 us

profile of v2, /device:TPU:0, one launch (start us, length us, event | category | flops | bytes accessed | tf_op | source)
XLA Modules:
  0.0 124.2 jit_solution(18234124991987253094)
XLA Ops:
  0.6 0.0 copy-start
  0.6 0.7 copy-done
  1.3 9.8 %updates.1 = (bf16[256,8192]{1,0:T(8,128)(2,1)S(1)}, bf16[256,8192]{1,0:T(8,128)(2,1)S(1)}, f32[2,64,8,128]{3,2,1,0:T(8,128)S(1)}) custom-call(bf16[1024,8192]{1,0:T(8,128)(2,1)} %act_ref.1, bf16[2,1024,128]{2,1,0:T(8,128)(2,1)} %grads_ref.1, bf16[2,1,8192,128]{3,2,1,0:T(8,128)(2,1)} %error_ref.1, f32[2,8,128]{2,1,0:T(8,128)S(1)} %bitcast.10), custom_call_target="tpu_custom_call" | custom-call | tf_op jit(solution)/shard_map/updates/pallas_call | solution.py:109
  11.1 24.5 %all_to_all.30.parts_ref = f32[128,8,128]{2,1,0:T(8,128)S(1)} all-to-all(f32[128,8,128]{2,1,0:T(8,128)S(1)} %bitcast.9), channel_id=1, replica_groups=mesh['dp'=16,'tensor'=8] {'dp','tensor'}, dimensions={0} | all-to-all | bytes 1048576 | tf_op jit(solution)/shard_map/all_to_all | solution.py:204
  35.5 0.2 spread.2
  35.7 18.0 %all_to_all.31 = f32[128,8,128]{2,1,0:T(8,128)S(1)} all-to-all(f32[128,8,128]{2,1,0:T(8,128)S(1)} %spread.2), channel_id=1, replica_groups=mesh['dp'=16,'tensor'=8] {'dp','tensor'}, dimensions={0} | all-to-all | bytes 1048576 | tf_op jit(solution)/shard_map/all_to_all | solution.py:208
  53.8 3.4 %right.2 = f32[16,2,8,128]{3,2,1,0:T(8,128)S(1)} custom-call(f32[2,64,8,128]{3,2,1,0:T(8,128)S(1)} %bitcast.7, bf16[256,8192]{1,0:T(8,128)(2,1)S(1)} %get-tuple-element.6.high_ref, bf16[256,8192]{1,0:T(8,128)(2,1)S(1)} %get-tuple-element.7.low_ref), custom_call_target="tpu_custom_call" | custom-call | tf_op jit(solution)/shard_map/right/pallas_call | solution.py:149
  57.1 10.5 %all_to_all.32.parts_ref = f32[16,2,8,128]{3,2,1,0:T(8,128)S(1)} all-to-all(f32[16,2,8,128]{3,2,1,0:T(8,128)S(1)} %right.2), channel_id=1, replica_groups=mesh['dp'=16,'tensor'=8] {'dp'}, dimensions={0} | all-to-all | bytes 262144 | tf_op jit(solution)/shard_map/all_to_all | solution.py:261
  67.6 1.3 %left.1 = f32[2,64,8,128]{3,2,1,0:T(8,128)S(1)} custom-call(f32[16,2,8,128]{3,2,1,0:T(8,128)S(1)} %all_to_all.32.parts_ref, bf16[256,8192]{1,0:T(8,128)(2,1)S(1)} %get-tuple-element.6.high_ref, bf16[256,8192]{1,0:T(8,128)(2,1)S(1)} %get-tuple-element.7.low_ref), custom_call_target="tpu_custom_call" | custom-call | tf_op jit(solution)/shard_map/left/pallas_call | solution.py:174
  69.0 18.8 %all_to_all.33.parts_ref = f32[128,8,128]{2,1,0:T(8,128)S(1)} all-to-all(f32[128,8,128]{2,1,0:T(8,128)S(1)} %bitcast.8), channel_id=1, replica_groups=mesh['dp'=16,'tensor'=8] {'dp','tensor'}, dimensions={0} | all-to-all | bytes 1048576 | tf_op jit(solution)/shard_map/all_to_all | solution.py:204
  87.8 0.2 spread.3
  87.9 18.0 %all_to_all.34 = f32[128,8,128]{2,1,0:T(8,128)S(1)} all-to-all(f32[128,8,128]{2,1,0:T(8,128)S(1)} %spread.3), channel_id=1, replica_groups=mesh['dp'=16,'tensor'=8] {'dp','tensor'}, dimensions={0} | all-to-all | bytes 1048576 | tf_op jit(solution)/shard_map/all_to_all | solution.py:208
  106.0 3.8 %right.3 = f32[16,2,8,128]{3,2,1,0:T(8,128)S(1)} custom-call(f32[2,64,8,128]{3,2,1,0:T(8,128)S(1)} %bitcast.5, bf16[256,8192]{1,0:T(8,128)(2,1)S(1)} %get-tuple-element.6.high_ref, bf16[256,8192]{1,0:T(8,128)(2,1)S(1)} %get-tuple-element.7.low_ref), custom_call_target="tpu_custom_call" | custom-call | tf_op jit(solution)/shard_map/right/pallas_call | solution.py:149
  109.8 10.5 %all_to_all.35.parts_ref = f32[16,2,8,128]{3,2,1,0:T(8,128)S(1)} all-to-all(f32[16,2,8,128]{3,2,1,0:T(8,128)S(1)} %right.3), channel_id=1, replica_groups=mesh['dp'=16,'tensor'=8] {'dp'}, dimensions={0} | all-to-all | bytes 262144 | tf_op jit(solution)/shard_map/all_to_all | solution.py:263
  120.3 3.8 %final.1 = (bf16[2,512,128]{2,1,0:T(8,128)(2,1)}, bf16[2,1,8192,128]{3,2,1,0:T(8,128)(2,1)}) custom-call(f32[16,2,8,128]{3,2,1,0:T(8,128)S(1)} %all_to_all.35.parts_ref, f32[2,64,8,128]{3,2,1,0:T(8,128)S(1)} %bitcast.6, bf16[256,8192]{1,0:T(8,128)(2,1)S(1)} %get-tuple-element.6.high_ref, bf16[256,8192]{1,0:T(8,128)(2,1)S(1)} %get-tuple-element.7.low_ref), custom_call_target="tpu_custom_call" | custom-call | tf_op jit(solution)/shard_map/final/pallas_call | solution.py:243
Async XLA Ops:
  0.6 0.7 copy-start

commit v3 on v2

v3 whole, which is shorter than its diff:
```python
import functools

import jax
import jax.numpy as jnp
from jax import lax
from jax.experimental import pallas as pl
from jax.experimental.pallas import tpu as pltpu
from jax.sharding import Mesh, PartitionSpec as P

RANK = 8
CHUNK = 1024
LANES = 128
F32, BF16 = jnp.float32, jnp.bfloat16
HIGHEST = lax.Precision.HIGHEST
NN = (((1,), (0,)), ((), ()))
NT = (((1,), (1,)), ((), ()))
TN = (((0,), (0,)), ((), ()))
WHOLE = pl.BlockSpec(memory_space=pltpu.VMEM)
in_vmem = functools.partial(pltpu.with_memory_space_constraint, memory_space=pltpu.VMEM)
in_hbm = functools.partial(pltpu.with_memory_space_constraint, memory_space=pltpu.HBM)


def params(mebibytes):
    return pltpu.CompilerParams(vmem_limit_bytes=mebibytes << 20)


def split(x):
    high = x.astype(BF16)
    return high, (x - high.astype(F32)).astype(BF16)


def dot(x, y, dims=NN):
    return lax.dot_general(x, y, dims, preferred_element_type=F32)


def exact_dot(x, y, dims=NN):
    return lax.dot_general(x, y, dims, precision=HIGHEST, preferred_element_type=F32)


def two_terms(x):
    return jnp.concatenate(split(x), axis=0)


def folded(pair):
    half = pair.shape[0] // 2
    return pair[:half] + pair[half:]


def store_tiles(out_ref, terms, first=0):
    for b in range(terms.shape[1] // LANES):
        for m in range(2):
            out_ref[first + b, m] = terms[m * RANK : (m + 1) * RANK, b * LANES : (b + 1) * LANES]


def rows_of(tiles_ref, first=0, count=None):
    count = tiles_ref.shape[0] if count is None else count
    return jnp.concatenate([tiles_ref[first + b] for b in range(count)], axis=1)


def own_matrix():
    return lax.axis_index("core")


def rows_at(m):
    return pl.ds(pl.multiple_of(m * LANES, LANES), LANES)


def updates_kernel(chunk, act_ref, grads_ref, error_ref, rows_ref, high_ref, low_ref, term_ref, act, grads, errors, rows, sems):
    tokens, d = act.shape
    parts = [pl.ds(first, chunk) for first in range(0, d, chunk)]
    grads_copy = pltpu.make_async_copy(grads_ref, grads, sems.at[0])
    rows_copy = pltpu.make_async_copy(rows_ref, rows, sems.at[2 * len(parts) + 1])
    rows_copy.start()
    grads_copy.start()
    copies = []
    for i, part in enumerate(parts):
        copies.append(
            [
                pltpu.make_async_copy(error_ref.at[:, :, part], errors.at[:, :, part], sems.at[2 * i + 1]),
                pltpu.make_async_copy(act_ref.at[:, part], act.at[:, part], sems.at[2 * i + 2]),
            ]
        )
        for copy in copies[-1]:
            copy.start()
    rows_copy.wait()
    warm = [two_terms(rows[m]) for m in range(2)]
    identity = jnp.where(
        lax.broadcasted_iota(jnp.int32, (LANES, LANES), 0) == lax.broadcasted_iota(jnp.int32, (LANES, LANES), 1), 1.0, 0.0
    ).astype(BF16)
    turn = [jnp.concatenate([identity, warm[m]], axis=0) for m in range(2)]
    grads_copy.wait()
    taken = two_terms(jnp.concatenate([folded(dot(warm[m], grads[m], NT)) for m in range(2)], axis=0))
    weights = jnp.concatenate([grads[0].T, grads[1].T, taken], axis=0)
    wide = 2 * LANES
    for i, part in enumerate(parts):
        for copy in copies[i]:
            copy.wait()
        turned = [dot(turn[m], errors[m, 0, part], NT) for m in range(2)]
        products = dot(weights, act[:, part])
        high, low = split(products[:wide] + jnp.concatenate([t[:LANES] for t in turned], axis=0))
        high_ref[:, part] = high
        low_ref[:, part] = low
        terms = jnp.concatenate([folded(t[LANES:]) for t in turned], axis=0)
        store_tiles(term_ref, folded(products[wide:]) + terms, i * chunk // LANES)


def make_updates(activations, output_grads, error_feedback, warm_rows):
    tokens, d = activations.shape
    chunk = min(CHUNK, d)
    wide = 2 * LANES
    loaded = (activations, output_grads, error_feedback, warm_rows)
    return pl.pallas_call(
        functools.partial(updates_kernel, chunk),
        in_specs=[pl.BlockSpec(memory_space=pl.ANY)] * 4,
        out_specs=[WHOLE] * 3,
        out_shape=[pltpu.VMEM((wide, d), BF16)] * 2 + [jax.ShapeDtypeStruct((d // LANES, 2, RANK, LANES), F32)],
        scratch_shapes=[pltpu.VMEM(x.shape, x.dtype) for x in loaded] + [pltpu.SemaphoreType.DMA((2 + 2 * (d // chunk),))],
        compiler_params=params(32),
        name="updates",
    )(*map(in_hbm, loaded))


def inverse_of_factor(gram):
    row = lax.broadcasted_iota(jnp.int32, (RANK, 2 * RANK), 0)
    column = lax.broadcasted_iota(jnp.int32, (RANK, 2 * RANK), 1)
    table = jnp.concatenate([gram, jnp.zeros_like(gram)], axis=1)
    table = jnp.where(column == row + RANK, jnp.float32(1), table)
    pivots = jnp.zeros((RANK, 2 * RANK), F32)
    for k in range(RANK):
        along = jnp.broadcast_to(table[:, k : k + 1], table.shape)
        pivot = jnp.broadcast_to(along[k : k + 1, :], table.shape)
        pivots = jnp.where(row == k, pivot, pivots)
        table = jnp.where(row > k, table - (along / pivot) * table[k : k + 1, :], table)
    return (table * (1.0 / jnp.sqrt(pivots)))[:, RANK:]


def right_rows(last, m, tiles_ref, high_ref, low_ref):
    rows = rows_of(tiles_ref)
    first, second = split(rows)
    third = (rows - first.astype(F32) - second.astype(F32)).astype(BF16)
    three = jnp.concatenate([first, second, third], axis=0)
    gram = dot(three, three, NT)
    gram = sum(gram[i * RANK : (i + 1) * RANK] for i in range(3))
    gram = sum(gram[:, i * RANK : (i + 1) * RANK] for i in range(3))
    part = rows_at(m)
    right = folded(dot(three[: 2 * RANK], high_ref[part, :], NT)) + dot(first, low_ref[part, :], NT)
    inverse = inverse_of_factor(gram)
    if last:
        inverse = exact_dot(inverse, inverse, TN)
    return exact_dot(inverse, right)


def right_own_kernel(last, tiles_ref, high_ref, low_ref, out_ref):
    out_ref[...] = right_rows(last, own_matrix(), tiles_ref, high_ref, low_ref)


def right_both_kernel(last, mine_ref, tiles_ref, high_ref, low_ref, out_ref):
    own = own_matrix()
    mine = mine_ref[...]
    other = right_rows(last, 1 - own, tiles_ref, high_ref, low_ref)
    for copy in range(out_ref.shape[0]):
        out_ref[copy, own] = mine
        out_ref[copy, 1 - own] = other


def right_terms(last, copies, tiles, high, low):
    other = lax.ppermute(tiles, "core", [(0, 1), (1, 0)])
    shared = dict(out_specs=WHOLE, compiler_params=params(24))
    mine = pl.pallas_call(
        functools.partial(right_own_kernel, last),
        in_specs=[WHOLE] * 3,
        out_shape=jax.ShapeDtypeStruct((RANK, LANES), F32),
        name="right_own",
        **shared,
    )(tiles, in_vmem(high), in_vmem(low))
    both = pl.pallas_call(
        functools.partial(right_both_kernel, last),
        in_specs=[WHOLE] * 4,
        out_shape=jax.ShapeDtypeStruct((copies, 2, RANK, LANES), F32),
        name="right_both",
        **shared,
    )(mine, other, in_vmem(high), in_vmem(low))
    return both, other


def total(parts_ref, m):
    return sum(parts_ref[r, m] for r in range(parts_ref.shape[0]))


def left_kernel(mine, parts_ref, high_ref, low_ref, term_ref):
    m = own_matrix() if mine else 1 - own_matrix()
    part = rows_at(m)
    f_high, f_low = split(total(parts_ref, m))
    both = jnp.concatenate([f_high, f_low], axis=0)
    step = min(2048, high_ref.shape[1])
    for first in range(0, high_ref.shape[1], step):
        columns = pl.ds(first, step)
        terms = folded(dot(both, high_ref[part, columns])) + dot(f_high, low_ref[part, columns])
        for b in range(step // LANES):
            term_ref[first // LANES + b] = terms[:, b * LANES : (b + 1) * LANES]


def left_terms(mine, parts, high, low):
    return pl.pallas_call(
        functools.partial(left_kernel, mine),
        in_specs=[WHOLE] * 3,
        out_specs=WHOLE,
        out_shape=jax.ShapeDtypeStruct((high.shape[1] // LANES, RANK, LANES), F32),
        compiler_params=params(24),
        name="left_own" if mine else "left_other",
    )(parts, in_vmem(high), in_vmem(low))


def add_kernel(x_ref, y_ref, out_ref):
    out_ref[...] = x_ref[...] + y_ref[...]


def chip_terms(parts, high, low):
    sent = lax.ppermute(left_terms(False, parts, high, low), "core", [(0, 1), (1, 0)])
    kept = left_terms(True, parts, high, low)
    return pl.pallas_call(
        add_kernel,
        in_specs=[WHOLE] * 2,
        out_specs=WHOLE,
        out_shape=jax.ShapeDtypeStruct(kept.shape, F32),
        compiler_params=params(8),
        name="add",
    )(sent, kept)


def spread_kernel(parts_ref, out_ref):
    total = parts_ref[0]
    for r in range(1, parts_ref.shape[0]):
        total = total + parts_ref[r]
    for r in range(out_ref.shape[0]):
        out_ref[r] = total


def spread_sum(parts, copies):
    return pl.pallas_call(
        spread_kernel,
        in_specs=[WHOLE],
        out_specs=WHOLE,
        out_shape=jax.ShapeDtypeStruct((copies,) + parts.shape[1:], F32),
        compiler_params=params(8),
        name="spread",
    )(parts)


def sum_own(tiles, axes):
    copies = tiles.shape[0]
    parts = lax.all_to_all(tiles.reshape((-1,) + tiles.shape[-2:]), axes, 0, 0)
    return lax.all_to_all(spread_sum(parts, copies), ("dp", "x"), 0, 0)


def mean_columns(weights, tiles):
    w_high, w_low = split(weights)
    t_high, t_low = split(tiles)
    left = jnp.concatenate([w_high, w_high, w_low], axis=0)
    right = jnp.concatenate([t_high, t_low, t_high], axis=0)
    return dot(left, right, TN)


def final_kernel(replicas, block, parts_ref, mine_ref, other_ref, high_ref, low_ref, decoded_ref, error_ref, held, sems):
    weights = [total(parts_ref, m) / replicas for m in range(2)]
    own = own_matrix()

    def mean(m, first, count):
        mine, other = (rows_of(ref, first, count) for ref in (mine_ref, other_ref))
        return mean_columns(weights[m], jnp.where(own == m, mine, other))

    copies = []
    for i in range(high_ref.shape[1] // block):
        columns = pl.ds(i * block, block)
        for m in range(2):
            part = pl.ds(m * LANES, LANES)
            updates = high_ref[part, columns].astype(F32) + low_ref[part, columns].astype(F32)
            held[m, 0, columns] = (updates - mean(m, i * block // LANES, block // LANES)).astype(BF16).T
        copy = pltpu.make_async_copy(held.at[:, :, columns], error_ref.at[:, :, columns], sems.at[i])
        copy.start()
        copies.append(copy)
    count = decoded_ref.shape[1] // LANES
    for m in range(2):
        decoded_ref[m] = mean(m, lax.axis_index("dp") * count, count).T.astype(BF16)
    for copy in copies:
        copy.wait()


def final_outputs(replicas, parts, mine, other, high, low):
    d = high.shape[1]
    block = min(1024, d)
    return pl.pallas_call(
        functools.partial(final_kernel, replicas, block),
        in_specs=[WHOLE] * 5,
        out_specs=[WHOLE, pl.BlockSpec(memory_space=pl.ANY)],
        out_shape=[
            jax.ShapeDtypeStruct((2, d // replicas, LANES), BF16),
            jax.ShapeDtypeStruct((2, 1, d, LANES), BF16),
        ],
        scratch_shapes=[
            pltpu.VMEM((2, 1, d, LANES), BF16),
            pltpu.SemaphoreType.DMA((d // block,)),
        ],
        compiler_params=params(24),
        name="final",
    )(parts, mine, other, in_vmem(high), in_vmem(low))


def local(activations, output_grads, error_feedback, warm_start):
    replicas = lax.axis_size("dp")
    high, low, term = make_updates(activations, output_grads, error_feedback, jnp.swapaxes(warm_start, 1, 2))
    mine = sum_own(term, ("dp", "x", "core"))
    terms, other = right_terms(False, replicas, mine, high, low)
    parts = lax.all_to_all(terms, "dp", 0, 0)
    mine = sum_own(chip_terms(parts, high, low), ("dp", "x"))
    terms, other = right_terms(True, replicas, mine, high, low)
    parts = lax.all_to_all(terms, "dp", 0, 0)
    return tuple(final_outputs(replicas, parts, mine, other, high, low))


def solution(mesh):
    replicas, width = mesh.devices.shape
    split_mesh = Mesh(mesh.devices.reshape(replicas, width // 2, 2), ("dp", "x", "core"))
    tensor = ("x", "core")
    return jax.shard_map(
        local,
        mesh=split_mesh,
        in_specs=(P("dp", None), P(None, "dp", tensor), P(None, "dp", None, tensor), P(None, tensor, None)),
        out_specs=(P(None, "dp", tensor), P(None, "dp", None, tensor)),
        check_vma=False,
    )
```

time: 125 us -> 117 us (0.936)
  blocking collectives: 100 us -> 93 us
    all_to_all x6, blocking collectives: 100 us -> 93 us  [the longest x2 40.2 us: sum_own(): parts = lax.all_to_all(tiles.reshape((-1,) + tiles.shape[-2:]), axes, 0, 0)]
    pallas_call x3 -> x7, Pallas kernels: 8.5 us -> 7.97 us  [the longest x2 3.37 us: right_terms(): pl.pallas_call(functools.partial(right_both_kernel, last), in_specs=[WHOL...]
  transfers between devices with their start and end apart: 0 -> 3, of which waited for: 0 -> 1; matrix products, arithmetic and copies ran while one was open for 0% -> 0% of each run, Pallas kernels for 0% -> 3%
where the time goes in v3:
time: 117 us
  blocking collectives  93 us (79%)
  Pallas kernels  21.7 us (19%)
    all_to_all x2, blocking collectives, sum_own(): parts = lax.all_to_all(tiles.reshape((-1,) + tiles.shape[-2:]), axes, 0, 0)  40.2 us
    all_to_all x2, blocking collectives, sum_own(): return lax.all_to_all(spread_sum(parts, copies), ('dp', 'x'), 0, 0)  30.7 us
    all_to_all x2, blocking collectives, local(): parts = lax.all_to_all(terms, 'dp', 0, 0)  22.1 us
    pallas_call x1, Pallas kernels, make_updates(): pl.pallas_call(functools.partial(updates_kernel, chunk), in_specs=[pl.Blo...  9.78 us
    pallas_call x1, Pallas kernels, final_outputs(): pl.pallas_call(functools.partial(final_kernel, replicas, block), in_specs...  3.73 us
    pallas_call x2, Pallas kernels, right_terms(): pl.pallas_call(functools.partial(right_both_kernel, last), in_specs=[WHOL...  3.37 us
    pallas_call x2, Pallas kernels, right_terms(): pl.pallas_call(functools.partial(right_own_kernel, last), in_specs=[WHOLE...  3.27 us
  transfers between devices with their start and end apart: 3, of which 1 were waited for; matrix products, arithmetic and copies ran while one was open for 0% of the time, Pallas kernels for 3%

profile of v3, /device:TPU:0, one launch (start us, length us, event | category | flops | bytes accessed | tf_op | source)
XLA Modules:
  0.0 116.5 jit_solution(698679491553136989)
XLA Ops:
  0.6 9.8 %updates.1 = (bf16[256,8192]{1,0:T(8,128)(2,1)S(1)}, bf16[256,8192]{1,0:T(8,128)(2,1)S(1)}, f32[64,2,8,128]{3,2,1,0:T(8,128)S(1)}) custom-call(bf16[1024,8192]{1,0:T(8,128)(2,1)} %act_ref.1, bf16[2,1024,128]{2,1,0:T(8,128)(2,1)} %grads_ref.1, bf16[2,1,8192,128]{3,2,1,0:T(8,128)(2,1)} %error_ref.1, f32[2,8,128]{2,1,0:T(8,128)} %bitcast.3), custom_call_target="tpu_custom_call" | custom-call | tf_op jit(solution)/shard_map/updates/pallas_call | solution.py:112
  10.4 24.5 %all_to_all.30.parts_ref = f32[128,8,128]{2,1,0:T(8,128)S(1)} all-to-all(f32[128,8,128]{2,1,0:T(8,128)S(1)} %bitcast.2), channel_id=1, replica_groups=mesh['dp'=16,'x'=4,'core'=2] {'dp','x','core'}, dimensions={0} | all-to-all | bytes 1048576 | tf_op jit(solution)/shard_map/all_to_all | solution.py:252
  34.9 0.2 spread.2
  35.0 15.5 %all_to_all.31.tiles_ref = f32[64,8,128]{2,1,0:T(8,128)S(1)} all-to-all(f32[64,8,128]{2,1,0:T(8,128)S(1)} %spread.2), channel_id=1, replica_groups=mesh['dp'=16,'x'=4,'core'=2] {'dp','x'}, dimensions={0} | all-to-all | bytes 524288 | tf_op jit(solution)/shard_map/all_to_all | solution.py:253
  50.5 0.0 collective-permute-start
  50.5 1.5 %right_own.2.mine_ref = f32[8,128]{1,0:T(8,128)S(1)} custom-call(f32[64,8,128]{2,1,0:T(8,128)S(1)} %all_to_all.31.tiles_ref, bf16[256,8192]{1,0:T(8,128)(2,1)S(1)} %get-tuple-element.6.high_ref, bf16[256,8192]{1,0:T(8,128)(2,1)S(1)} %get-tuple-element.7.low_ref), custom_call_target="tpu_custom_call" | custom-call | tf_op jit(solution)/shard_map/right_own/pallas_call | solution.py:169
  52.1 0.0 collective-permute-done.tiles_ref
  52.1 1.6 %right_both.2 = f32[16,2,8,128]{3,2,1,0:T(8,128)S(1)} custom-call(f32[8,128]{1,0:T(8,128)S(1)} %right_own.2.mine_ref, f32[64,8,128]{2,1,0:T(8,128)S(1)} %collective-permute-done.tiles_ref, bf16[256,8192]{1,0:T(8,128)(2,1)S(1)} %get-tuple-element.6.high_ref, bf16[256,8192]{1,0:T(8,128)(2,1)S(1)} %get-tuple-element.7.low_ref), custom_call_target="tpu_custom_call" | custom-call | tf_op jit(solution)/shard_map/right_both/pallas_call | solution.py:176
  53.6 11.0 %all_to_all.32.parts_ref = f32[16,2,8,128]{3,2,1,0:T(8,128)S(1)} all-to-all(f32[16,2,8,128]{3,2,1,0:T(8,128)S(1)} %right_both.2), channel_id=1, replica_groups=mesh['dp'=16,'x'=4,'core'=2] {'dp'}, dimensions={0} | all-to-all | bytes 262144 | tf_op jit(solution)/shard_map/all_to_all | solution.py:314
  64.7 0.7 left_other.1
  65.3 0.1 collective-permute-start.1
  65.4 0.7 left_own.1.y_ref
  66.1 0.9 collective-permute-done.1.x_ref
  67.0 15.8 %all_to_all.33.parts_ref = f32[64,8,128]{2,1,0:T(8,128)S(1)} all-to-all(f32[64,8,128]{2,1,0:T(8,128)S(1)} %add.1), channel_id=1, replica_groups=mesh['dp'=16,'x'=4,'core'=2] {'dp','x'}, dimensions={0} | all-to-all | bytes 524288 | tf_op jit(solution)/shard_map/all_to_all | solution.py:252
  82.7 0.1 spread.3
  82.8 15.3 %all_to_all.34.tiles_ref.mine_ref = f32[64,8,128]{2,1,0:T(8,128)S(1)} all-to-all(f32[64,8,128]{2,1,0:T(8,128)S(1)} %spread.3), channel_id=1, replica_groups=mesh['dp'=16,'x'=4,'core'=2] {'dp','x'}, dimensions={0} | all-to-all | bytes 524288 | tf_op jit(solution)/shard_map/all_to_all | solution.py:253
  98.1 0.0 collective-permute-start.2
  98.1 1.7 %right_own.3.mine_ref = f32[8,128]{1,0:T(8,128)S(1)} custom-call(f32[64,8,128]{2,1,0:T(8,128)S(1)} %all_to_all.34.tiles_ref.mine_ref, bf16[256,8192]{1,0:T(8,128)(2,1)S(1)} %get-tuple-element.6.high_ref, bf16[256,8192]{1,0:T(8,128)(2,1)S(1)} %get-tuple-element.7.low_ref), custom_call_target="tpu_custom_call" | custom-call | tf_op jit(solution)/shard_map/right_own/pallas_call | solution.py:169
  99.8 0.0 collective-permute-done.2.tiles_ref.other_ref
  99.8 1.8 %right_both.3 = f32[16,2,8,128]{3,2,1,0:T(8,128)S(1)} custom-call(f32[8,128]{1,0:T(8,128)S(1)} %right_own.3.mine_ref, f32[64,8,128]{2,1,0:T(8,128)S(1)} %collective-permute-done.2.tiles_ref.other_ref, bf16[256,8192]{1,0:T(8,128)(2,1)S(1)} %get-tuple-element.6.high_ref, bf16[256,8192]{1,0:T(8,128)(2,1)S(1)} %get-tuple-element.7.low_ref), custom_call_target="tpu_custom_call" | custom-call | tf_op jit(solution)/shard_map/right_both/pallas_call | solution.py:176
  101.6 11.0 %all_to_all.35.parts_ref = f32[16,2,8,128]{3,2,1,0:T(8,128)S(1)} all-to-all(f32[16,2,8,128]{3,2,1,0:T(8,128)S(1)} %right_both.3), channel_id=1, replica_groups=mesh['dp'=16,'x'=4,'core'=2] {'dp'}, dimensions={0} | all-to-all | bytes 262144 | tf_op jit(solution)/shard_map/all_to_all | solution.py:317
  112.6 3.7 %final.1 = (bf16[2,512,128]{2,1,0:T(8,128)(2,1)}, bf16[2,1,8192,128]{3,2,1,0:T(8,128)(2,1)}) custom-call(f32[16,2,8,128]{3,2,1,0:T(8,128)S(1)} %all_to_all.35.parts_ref, f32[64,8,128]{2,1,0:T(8,128)S(1)} %all_to_all.34.tiles_ref.mine_ref, f32[64,8,128]{2,1,0:T(8,128)S(1)} %collective-permute-done.2.tiles_ref.other_ref, ...), custom_call_target="tpu_custom_call" | custom-call | tf_op jit(solution)/shard_map/final/pallas_call | solution.py:292
  (1 shorter events, 0.0 us)
Async XLA Ops:
  50.5 1.5 %collective-permute-start = (f32[64,8,128]{2,1,0:T(8,128)S(1)}, f32[64,8,128]{2,1,0:T(8,128)S(1)}, u32[]{:S(2)}, u32[]{:S(2)}) collective-permute-start(f32[64,8,128]{2,1,0:T(8,128)S(1)} %all_to_all.31.tiles_ref), channel_id=1, source_target_pairs={{0,1},{1,0},{2,3},{3,2},{4,5},{5,4},{6,7},{7,6},{8,9},{9,8},{10,11... | collective-permute-start | bytes 786440 | tf_op jit(solution)/shard_map/ppermute | solution.py:167
  65.3 1.6 %collective-permute-start.1 = (f32[64,8,128]{2,1,0:T(8,128)S(1)}, f32[64,8,128]{2,1,0:T(8,128)S(1)}, u32[]{:S(2)}, u32[]{:S(2)}) collective-permute-start(f32[64,8,128]{2,1,0:T(8,128)S(1)} %left_other.1), channel_id=1, source_target_pairs={{0,1},{1,0},{2,3},{3,2},{4,5},{5,4},{6,7},{7,6},{8,9},{9,8},{10,11... | collective-permute-start | bytes 786440 | tf_op jit(solution)/shard_map/ppermute | solution.py:219
  98.1 1.7 %collective-permute-start.2 = (f32[64,8,128]{2,1,0:T(8,128)S(1)}, f32[64,8,128]{2,1,0:T(8,128)S(1)}, u32[]{:S(2)}, u32[]{:S(2)}) collective-permute-start(f32[64,8,128]{2,1,0:T(8,128)S(1)} %all_to_all.34.tiles_ref.mine_ref), channel_id=1, source_target_pairs={{0,1},{1,0},{2,3},{3,2},{4,5},{5,4},{6,7},{7,6},{8,9},{9,8},{10,11... | collective-permute-start | bytes 786440 | tf_op jit(solution)/shard_map/ppermute | solution.py:167

commit v4 on v3

--- a/solution.py
+++ b/solution.py
@@ -9,6 +9,7 @@
 
 RANK = 8
 CHUNK = 1024
+STEP = 256
 LANES = 128
 F32, BF16 = jnp.float32, jnp.bfloat16
 HIGHEST = lax.Precision.HIGHEST
@@ -46,12 +47,6 @@
     return pair[:half] + pair[half:]
 
 
-def store_tiles(out_ref, terms, first=0):
-    for b in range(terms.shape[1] // LANES):
-        for m in range(2):
-            out_ref[first + b, m] = terms[m * RANK : (m + 1) * RANK, b * LANES : (b + 1) * LANES]
-
-
 def rows_of(tiles_ref, first=0, count=None):
     count = tiles_ref.shape[0] if count is None else count
     return jnp.concatenate([tiles_ref[first + b] for b in range(count)], axis=1)
@@ -65,59 +60,113 @@
     return pl.ds(pl.multiple_of(m * LANES, LANES), LANES)
 
 
-def updates_kernel(chunk, act_ref, grads_ref, error_ref, rows_ref, high_ref, low_ref, term_ref, act, grads, errors, rows, sems):
-    tokens, d = act.shape
-    parts = [pl.ds(first, chunk) for first in range(0, d, chunk)]
-    grads_copy = pltpu.make_async_copy(grads_ref, grads, sems.at[0])
-    rows_copy = pltpu.make_async_copy(rows_ref, rows, sems.at[2 * len(parts) + 1])
+def transposed_updates(weights, act, errors):
+    products = dot(weights, act)
+    turned = [e.T for e in errors]
+    wide = 2 * LANES
+    return split(products[:wide] + jnp.concatenate(turned, axis=0).astype(F32)), products[wide:], turned
+
+
+def updates_kernel(chunk, head, act_ref, grads_ref, error_ref, rows_ref, high_ref, low_ref, send_ref, keep_ref, tail_act, tail_errors, grads_t, act, grads, errors, rows, sems):
+    d = high_ref.shape[1]
+    rows_copy = pltpu.make_async_copy(rows_ref, rows, sems.at[0])
+    grads_copy = pltpu.make_async_copy(grads_ref, grads, sems.at[1])
     rows_copy.start()
     grads_copy.start()
-    copies = []
-    for i, part in enumerate(parts):
-        copies.append(
-            [
-                pltpu.make_async_copy(error_ref.at[:, :, part], errors.at[:, :, part], sems.at[2 * i + 1]),
-                pltpu.make_async_copy(act_ref.at[:, part], act.at[:, part], sems.at[2 * i + 2]),
-            ]
-        )
-        for copy in copies[-1]:
+    places, copies = [], []
+    for i in range(d // chunk):
+        part = pl.ds(i * chunk, chunk)
+        here = part if i < head else pl.ds((i - head) * chunk, chunk)
+        act_at, error_at = (act, errors) if i < head else (tail_act, tail_errors)
+        pair = [
+            pltpu.make_async_copy(error_ref.at[:, :, part], error_at.at[:, :, here], sems.at[2 * i + 2]),
+            pltpu.make_async_copy(act_ref.at[:, part], act_at.at[:, here], sems.at[2 * i + 3]),
+        ]
+        for copy in pair:
             copy.start()
+        copies.append(pair)
+        places.append((act_at, error_at, 0 if i < head else head * chunk))
     rows_copy.wait()
     warm = [two_terms(rows[m]) for m in range(2)]
-    identity = jnp.where(
-        lax.broadcasted_iota(jnp.int32, (LANES, LANES), 0) == lax.broadcasted_iota(jnp.int32, (LANES, LANES), 1), 1.0, 0.0
-    ).astype(BF16)
-    turn = [jnp.concatenate([identity, warm[m]], axis=0) for m in range(2)]
     grads_copy.wait()
     taken = two_terms(jnp.concatenate([folded(dot(warm[m], grads[m], NT)) for m in range(2)], axis=0))
-    weights = jnp.concatenate([grads[0].T, grads[1].T, taken], axis=0)
     wide = 2 * LANES
-    for i, part in enumerate(parts):
-        for copy in copies[i]:
+    for m in range(2):
+        grads_t[m * LANES : (m + 1) * LANES] = grads[m].T
+    weights = jnp.concatenate([grads_t[...], taken], axis=0)
+    first_core = own_matrix() == 0
+    step = min(STEP, chunk)
+    for i, pair in enumerate(copies):
+        act_at, error_at, shift = places[i]
+        for copy in pair:
             copy.wait()
-        turned = [dot(turn[m], errors[m, 0, part], NT) for m in range(2)]
-        products = dot(weights, act[:, part])
-        high, low = split(products[:wide] + jnp.concatenate([t[:LANES] for t in turned], axis=0))
+        for first in range(i * chunk, (i + 1) * chunk, step):
+            here = pl.ds(first - shift, step)
+            if i < head:
+                part = pl.ds(first, step)
+                (high, low), left, turned = transposed_updates(weights, act_at[:, here], [error_at[m, 0, here] for m in range(2)])
+                high_ref[:, part] = high
+                low_ref[:, part] = low
+                moved = [dot(warm[m], turned[m]) for m in range(2)]
+            else:
+                left = dot(taken, act_at[:, here])
+                moved = [dot(warm[m], error_at[m, 0, here], NT) for m in range(2)]
+            terms = folded(left) + jnp.concatenate([folded(x) for x in moved], axis=0)
+            key, value = terms[:RANK], terms[RANK:]
+            keep, send = jnp.where(first_core, key, value), jnp.where(first_core, value, key)
+            for b in range(step // LANES):
+                keep_ref[first // LANES + b] = keep[:, b * LANES : (b + 1) * LANES]
+                send_ref[first // LANES + b] = send[:, b * LANES : (b + 1) * LANES]
+
+
+def tail_kernel(act_ref, error_ref, grads_t, keep_in, high_in, low_in, high_ref, low_ref, keep_ref):
+    keep_ref[...] = keep_in[...]
+    count = act_ref.shape[1]
+    step = min(STEP, count)
+    for first in range(0, count, step):
+        here = pl.ds(first, step)
+        part = pl.ds(high_ref.shape[1] - count + first, step)
+        (high, low), _, _ = transposed_updates(grads_t[...], act_ref[:, here], [error_ref[m, 0, here] for m in range(2)])
         high_ref[:, part] = high
         low_ref[:, part] = low
-        terms = jnp.concatenate([folded(t[LANES:]) for t in turned], axis=0)
-        store_tiles(term_ref, folded(products[wide:]) + terms, i * chunk // LANES)
 
 
 def make_updates(activations, output_grads, error_feedback, warm_rows):
     tokens, d = activations.shape
     chunk = min(CHUNK, d)
-    wide = 2 * LANES
+    count = d // chunk
+    head = max(1, 3 * count // 4)
+    wide, early, late = 2 * LANES, head * chunk, (count - head) * chunk
     loaded = (activations, output_grads, error_feedback, warm_rows)
-    return pl.pallas_call(
-        functools.partial(updates_kernel, chunk),
+    tiles = jax.ShapeDtypeStruct((d // LANES, RANK, LANES), F32)
+    whole = [pltpu.VMEM((wide, d), BF16)] * 2
+    high, low, send, keep, act, errors, grads_t = pl.pallas_call(
+        functools.partial(updates_kernel, chunk, head),
         in_specs=[pl.BlockSpec(memory_space=pl.ANY)] * 4,
-        out_specs=[WHOLE] * 3,
-        out_shape=[pltpu.VMEM((wide, d), BF16)] * 2 + [jax.ShapeDtypeStruct((d // LANES, 2, RANK, LANES), F32)],
-        scratch_shapes=[pltpu.VMEM(x.shape, x.dtype) for x in loaded] + [pltpu.SemaphoreType.DMA((2 + 2 * (d // chunk),))],
-        compiler_params=params(32),
+        out_specs=[WHOLE] * 7,
+        out_shape=whole
+        + [tiles, tiles, pltpu.VMEM((tokens, late), BF16), pltpu.VMEM((2, 1, late, LANES), BF16), pltpu.VMEM((wide, tokens), BF16)],
+        scratch_shapes=[
+            pltpu.VMEM((tokens, early), BF16),
+            pltpu.VMEM(output_grads.shape, BF16),
+            pltpu.VMEM((2, 1, early, LANES), BF16),
+            pltpu.VMEM(warm_rows.shape, F32),
+            pltpu.SemaphoreType.DMA((2 + 2 * count,)),
+        ],
+        compiler_params=params(24),
         name="updates",
     )(*map(in_hbm, loaded))
+    sent = lax.ppermute(send, "core", [(0, 1), (1, 0)])
+    high, low, keep = pl.pallas_call(
+        tail_kernel,
+        in_specs=[WHOLE] * 6,
+        out_specs=[WHOLE] * 3,
+        out_shape=whole + [tiles],
+        input_output_aliases={4: 0, 5: 1},
+        compiler_params=params(8),
+        name="updates_tail",
+    )(*map(in_vmem, (act, errors, grads_t)), keep, in_vmem(high), in_vmem(low))
+    return high, low, added(sent, keep)
 
 
 def inverse_of_factor(gram):
@@ -215,17 +264,20 @@
     out_ref[...] = x_ref[...] + y_ref[...]
 
 
-def chip_terms(parts, high, low):
-    sent = lax.ppermute(left_terms(False, parts, high, low), "core", [(0, 1), (1, 0)])
-    kept = left_terms(True, parts, high, low)
+def added(x, y):
     return pl.pallas_call(
         add_kernel,
         in_specs=[WHOLE] * 2,
         out_specs=WHOLE,
-        out_shape=jax.ShapeDtypeStruct(kept.shape, F32),
+        out_shape=jax.ShapeDtypeStruct(x.shape, F32),
         compiler_params=params(8),
         name="add",
-    )(sent, kept)
+    )(x, y)
+
+
+def chip_terms(parts, high, low):
+    sent = lax.ppermute(left_terms(False, parts, high, low), "core", [(0, 1), (1, 0)])
+    return added(sent, left_terms(True, parts, high, low))
 
 
 def spread_kernel(parts_ref, out_ref):
@@ -247,10 +299,9 @@
     )(parts)
 
 
-def sum_own(tiles, axes):
-    copies = tiles.shape[0]
-    parts = lax.all_to_all(tiles.reshape((-1,) + tiles.shape[-2:]), axes, 0, 0)
-    return lax.all_to_all(spread_sum(parts, copies), ("dp", "x"), 0, 0)
+def sum_own(tiles):
+    parts = lax.all_to_all(tiles, ("dp", "x"), 0, 0)
+    return lax.all_to_all(spread_sum(parts, tiles.shape[0]), ("dp", "x"), 0, 0)
 
 
 def mean_columns(weights, tiles):
@@ -309,10 +360,10 @@
 def local(activations, output_grads, error_feedback, warm_start):
     replicas = lax.axis_size("dp")
     high, low, term = make_updates(activations, output_grads, error_feedback, jnp.swapaxes(warm_start, 1, 2))
-    mine = sum_own(term, ("dp", "x", "core"))
+    mine = sum_own(term)
     terms, other = right_terms(False, replicas, mine, high, low)
     parts = lax.all_to_all(terms, "dp", 0, 0)
-    mine = sum_own(chip_terms(parts, high, low), ("dp", "x"))
+    mine = sum_own(chip_terms(parts, high, low))
     terms, other = right_terms(True, replicas, mine, high, low)
     parts = lax.all_to_all(terms, "dp", 0, 0)
     return tuple(final_outputs(replicas, parts, mine, other, high, low))

time: 117 us -> 115 us (0.983)
  blocking collectives: 93 us -> 90.9 us
    all_to_all x4, blocking collectives: 71 us -> 68.8 us  [the longest x2 38.3 us: sum_own(): parts = lax.all_to_all(tiles, ('dp', 'x'), 0, 0)]
    pallas_call x2 -> x4, Pallas kernels: 9.8 us -> 10.4 us  [the longest x1 8.81 us: make_updates(): pl.pallas_call(functools.partial(updates_kernel, chunk, head), in_specs=[...]
  transfers between devices with their start and end apart: 3 -> 4, of which waited for: 1 -> 1; matrix products, arithmetic and copies ran while one was open for 0% -> 0% of each run, Pallas kernels for 3% -> 5%
where the time goes in v4:
time: 115 us
  blocking collectives  90.9 us (79%)
  Pallas kernels  22.2 us (19%)
    all_to_all x2, blocking collectives, sum_own(): parts = lax.all_to_all(tiles, ('dp', 'x'), 0, 0)  38.3 us
    all_to_all x2, blocking collectives, sum_own(): return lax.all_to_all(spread_sum(parts, tiles.shape[0]), ('dp', 'x'), 0, 0)  30.5 us
    all_to_all x2, blocking collectives, local(): parts = lax.all_to_all(terms, 'dp', 0, 0)  22.1 us
    pallas_call x1, Pallas kernels, make_updates(): pl.pallas_call(functools.partial(updates_kernel, chunk, head), in_specs=[...  8.81 us
    pallas_call x1, Pallas kernels, final_outputs(): pl.pallas_call(functools.partial(final_kernel, replicas, block), in_specs...  3.71 us
    pallas_call x2, Pallas kernels, right_terms(): pl.pallas_call(functools.partial(right_both_kernel, last), in_specs=[WHOL...  3.37 us
    pallas_call x2, Pallas kernels, right_terms(): pl.pallas_call(functools.partial(right_own_kernel, last), in_specs=[WHOLE...  3.27 us
  transfers between devices with their start and end apart: 4, of which 1 were waited for; matrix products, arithmetic and copies ran while one was open for 0% of the time, Pallas kernels for 5%

profile of v4, /device:TPU:0, one launch (start us, length us, event | category | flops | bytes accessed | tf_op | source)
XLA Modules:
  0.0 115.0 jit_solution(17944296672743140603)
XLA Ops:
  0.6 8.8 %updates.1 = (bf16[256,8192]{1,0:T(8,128)(2,1)S(1)}, bf16[256,8192]{1,0:T(8,128)(2,1)S(1)}, f32[64,8,128]{2,1,0:T(8,128)S(1)}, f32[64,8,128]{2,1,0:T(8,128)S(1)}...) custom-call(bf16[1024,8192]{1,0:T(8,128)(2,1)} %act_ref.1, ...), custom_call_target="tpu_custom_call" | custom-call | tf_op jit(solution)/shard_map/updates/pallas_call | solution.py:143
  9.4 0.1 collective-permute-start
  9.5 1.5 %updates_tail.1 = (bf16[256,8192]{1,0:T(8,128)(2,1)S(1)}, bf16[256,8192]{1,0:T(8,128)(2,1)S(1)}, f32[64,8,128]{2,1,0:T(8,128)S(1)}) custom-call(bf16[1024,2048]{1,0:T(8,128)(2,1)S(1)} %get-tuple-element.13.act_ref, bf16[2,1,2048,128]{3,2,1,0:T(8,128)(2,1)S(1)} %get-tuple-element.14.error_ref, ...), custom_call_target="tpu_custom_call", output_to_operand_aliasing={{0}: (4, {}), {1}: (5, {})} | custom-call | tf_op jit(solution)/shard_map/updates_tail/pallas_call | solution.py:160
  11.0 0.0 collective-permute-done.x_ref
  11.1 22.5 %all_to_all.30.parts_ref = f32[64,8,128]{2,1,0:T(8,128)S(1)} all-to-all(f32[64,8,128]{2,1,0:T(8,128)S(1)} %add.2), channel_id=1, replica_groups=mesh['dp'=16,'x'=4,'core'=2] {'dp','x'}, dimensions={0} | all-to-all | bytes 524288 | tf_op jit(solution)/shard_map/all_to_all | solution.py:303
  33.6 0.1 spread.2
  33.7 15.3 %all_to_all.31.tiles_ref = f32[64,8,128]{2,1,0:T(8,128)S(1)} all-to-all(f32[64,8,128]{2,1,0:T(8,128)S(1)} %spread.2), channel_id=1, replica_groups=mesh['dp'=16,'x'=4,'core'=2] {'dp','x'}, dimensions={0} | all-to-all | bytes 524288 | tf_op jit(solution)/shard_map/all_to_all | solution.py:304
  49.0 0.0 collective-permute-start.1
  49.0 1.5 %right_own.2.mine_ref = f32[8,128]{1,0:T(8,128)S(1)} custom-call(f32[64,8,128]{2,1,0:T(8,128)S(1)} %all_to_all.31.tiles_ref, bf16[256,8192]{1,0:T(8,128)(2,1)S(1)} %get-tuple-element.20.high_ref, bf16[256,8192]{1,0:T(8,128)(2,1)S(1)} %get-tuple-element.21.low_ref), custom_call_target="tpu_custom_call" | custom-call | tf_op jit(solution)/shard_map/right_own/pallas_call | solution.py:218
  50.5 0.0 collective-permute-done.1.tiles_ref
  50.5 1.6 %right_both.2 = f32[16,2,8,128]{3,2,1,0:T(8,128)S(1)} custom-call(f32[8,128]{1,0:T(8,128)S(1)} %right_own.2.mine_ref, f32[64,8,128]{2,1,0:T(8,128)S(1)} %collective-permute-done.1.tiles_ref, bf16[256,8192]{1,0:T(8,128)(2,1)S(1)} %get-tuple-element.20.high_ref, bf16[256,8192]{1,0:T(8,128)(2,1)S(1)} %get-tuple-element.21.low_ref), custom_call_target="tpu_custom_call" | custom-call | tf_op jit(solution)/shard_map/right_both/pallas_call | solution.py:225
  52.1 11.0 %all_to_all.32.parts_ref = f32[16,2,8,128]{3,2,1,0:T(8,128)S(1)} all-to-all(f32[16,2,8,128]{3,2,1,0:T(8,128)S(1)} %right_both.2), channel_id=1, replica_groups=mesh['dp'=16,'x'=4,'core'=2] {'dp'}, dimensions={0} | all-to-all | bytes 262144 | tf_op jit(solution)/shard_map/all_to_all | solution.py:365
  63.2 0.7 left_other.1
  63.8 0.1 collective-permute-start.2
  63.9 0.7 left_own.1.y_ref
  64.5 0.9 collective-permute-done.2.x_ref
  65.4 15.8 %all_to_all.33.parts_ref = f32[64,8,128]{2,1,0:T(8,128)S(1)} all-to-all(f32[64,8,128]{2,1,0:T(8,128)S(1)} %add.3), channel_id=1, replica_groups=mesh['dp'=16,'x'=4,'core'=2] {'dp','x'}, dimensions={0} | all-to-all | bytes 524288 | tf_op jit(solution)/shard_map/all_to_all | solution.py:303
  81.2 0.1 spread.3
  81.3 15.3 %all_to_all.34.tiles_ref.mine_ref = f32[64,8,128]{2,1,0:T(8,128)S(1)} all-to-all(f32[64,8,128]{2,1,0:T(8,128)S(1)} %spread.3), channel_id=1, replica_groups=mesh['dp'=16,'x'=4,'core'=2] {'dp','x'}, dimensions={0} | all-to-all | bytes 524288 | tf_op jit(solution)/shard_map/all_to_all | solution.py:304
  96.6 0.0 collective-permute-start.3
  96.6 1.7 %right_own.3.mine_ref = f32[8,128]{1,0:T(8,128)S(1)} custom-call(f32[64,8,128]{2,1,0:T(8,128)S(1)} %all_to_all.34.tiles_ref.mine_ref, bf16[256,8192]{1,0:T(8,128)(2,1)S(1)} %get-tuple-element.20.high_ref, bf16[256,8192]{1,0:T(8,128)(2,1)S(1)} %get-tuple-element.21.low_ref), custom_call_target="tpu_custom_call" | custom-call | tf_op jit(solution)/shard_map/right_own/pallas_call | solution.py:218
  98.3 0.0 collective-permute-done.3.tiles_ref.other_ref
  98.3 1.8 %right_both.3 = f32[16,2,8,128]{3,2,1,0:T(8,128)S(1)} custom-call(f32[8,128]{1,0:T(8,128)S(1)} %right_own.3.mine_ref, f32[64,8,128]{2,1,0:T(8,128)S(1)} %collective-permute-done.3.tiles_ref.other_ref, bf16[256,8192]{1,0:T(8,128)(2,1)S(1)} %get-tuple-element.20.high_ref, bf16[256,8192]{1,0:T(8,128)(2,1)S(1)} %get-tuple-element.21.low_ref), custom_call_target="tpu_custom_call" | custom-call | tf_op jit(solution)/shard_map/right_both/pallas_call | solution.py:225
  100.1 11.0 %all_to_all.35.parts_ref = f32[16,2,8,128]{3,2,1,0:T(8,128)S(1)} all-to-all(f32[16,2,8,128]{3,2,1,0:T(8,128)S(1)} %right_both.3), channel_id=1, replica_groups=mesh['dp'=16,'x'=4,'core'=2] {'dp'}, dimensions={0} | all-to-all | bytes 262144 | tf_op jit(solution)/shard_map/all_to_all | solution.py:368
  111.1 3.7 %final.1 = (bf16[2,512,128]{2,1,0:T(8,128)(2,1)}, bf16[2,1,8192,128]{3,2,1,0:T(8,128)(2,1)}) custom-call(f32[16,2,8,128]{3,2,1,0:T(8,128)S(1)} %all_to_all.35.parts_ref, f32[64,8,128]{2,1,0:T(8,128)S(1)} %all_to_all.34.tiles_ref.mine_ref, f32[64,8,128]{2,1,0:T(8,128)S(1)} %collective-permute-done.3.tiles_ref.other_ref, ...), custom_call_target="tpu_custom_call" | custom-call | tf_op jit(solution)/shard_map/final/pallas_call | solution.py:343
  (2 shorter events, 0.1 us)
Async XLA Ops:
  9.4 1.6 %collective-permute-start = (f32[64,8,128]{2,1,0:T(8,128)S(1)}, f32[64,8,128]{2,1,0:T(8,128)S(1)}, u32[]{:S(2)}, u32[]{:S(2)}) collective-permute-start(f32[64,8,128]{2,1,0:T(8,128)S(1)} %get-tuple-element.12), channel_id=1, source_target_pairs={{0,1},{1,0},{2,3},{3,2},{4,5},{5,4},{6,7},{7,6},{8,9},{9,8},{10,11... | collective-permute-start | bytes 786440 | tf_op jit(solution)/shard_map/ppermute | solution.py:159
  49.0 1.5 %collective-permute-start.1 = (f32[64,8,128]{2,1,0:T(8,128)S(1)}, f32[64,8,128]{2,1,0:T(8,128)S(1)}, u32[]{:S(2)}, u32[]{:S(2)}) collective-permute-start(f32[64,8,128]{2,1,0:T(8,128)S(1)} %all_to_all.31.tiles_ref), channel_id=1, source_target_pairs={{0,1},{1,0},{2,3},{3,2},{4,5},{5,4},{6,7},{7,6},{8,9},{9,8},{10,11... | collective-permute-start | bytes 786440 | tf_op jit(solution)/shard_map/ppermute | solution.py:216
  63.8 1.6 %collective-permute-start.2 = (f32[64,8,128]{2,1,0:T(8,128)S(1)}, f32[64,8,128]{2,1,0:T(8,128)S(1)}, u32[]{:S(2)}, u32[]{:S(2)}) collective-permute-start(f32[64,8,128]{2,1,0:T(8,128)S(1)} %left_other.1), channel_id=1, source_target_pairs={{0,1},{1,0},{2,3},{3,2},{4,5},{5,4},{6,7},{7,6},{8,9},{9,8},{10,11... | collective-permute-start | bytes 786440 | tf_op jit(solution)/shard_map/ppermute | solution.py:279
  96.6 1.7 %collective-permute-start.3 = (f32[64,8,128]{2,1,0:T(8,128)S(1)}, f32[64,8,128]{2,1,0:T(8,128)S(1)}, u32[]{:S(2)}, u32[]{:S(2)}) collective-permute-start(f32[64,8,128]{2,1,0:T(8,128)S(1)} %all_to_all.34.tiles_ref.mine_ref), channel_id=1, source_target_pairs={{0,1},{1,0},{2,3},{3,2},{4,5},{5,4},{6,7},{7,6},{8,9},{9,8},{10,11... | collective-permute-start | bytes 786440 | tf_op jit(solution)/shard_map/ppermute | solution.py:216

commit v5 on v4

--- a/solution.py
+++ b/solution.py
@@ -54,6 +54,10 @@
 
 def own_matrix():
     return lax.axis_index("core")
+
+
+def swapped(x):
+    return lax.ppermute(x, "core", [(0, 1), (1, 0)])
 
 
 def rows_at(m):
@@ -156,7 +160,7 @@
         compiler_params=params(24),
         name="updates",
     )(*map(in_hbm, loaded))
-    sent = lax.ppermute(send, "core", [(0, 1), (1, 0)])
+    sent = swapped(send)
     high, low, keep = pl.pallas_call(
         tail_kernel,
         in_specs=[WHOLE] * 6,
@@ -183,61 +187,71 @@
     return (table * (1.0 / jnp.sqrt(pivots)))[:, RANK:]
 
 
-def right_rows(last, m, tiles_ref, high_ref, low_ref):
-    rows = rows_of(tiles_ref)
-    first, second = split(rows)
-    third = (rows - first.astype(F32) - second.astype(F32)).astype(BF16)
-    three = jnp.concatenate([first, second, third], axis=0)
+def three_terms(x):
+    first, second = split(x)
+    return jnp.concatenate([first, second, (x - first.astype(F32) - second.astype(F32)).astype(BF16)], axis=0)
+
+
+def gram_of(three):
     gram = dot(three, three, NT)
     gram = sum(gram[i * RANK : (i + 1) * RANK] for i in range(3))
-    gram = sum(gram[:, i * RANK : (i + 1) * RANK] for i in range(3))
+    return sum(gram[:, i * RANK : (i + 1) * RANK] for i in range(3))
+
+
+def right_rows(last, m, three, gram, high_ref, low_ref):
     part = rows_at(m)
-    right = folded(dot(three[: 2 * RANK], high_ref[part, :], NT)) + dot(first, low_ref[part, :], NT)
+    right = folded(dot(three[: 2 * RANK], high_ref[part, :], NT)) + dot(three[:RANK], low_ref[part, :], NT)
+    if not last:
+        return right
     inverse = inverse_of_factor(gram)
-    if last:
-        inverse = exact_dot(inverse, inverse, TN)
-    return exact_dot(inverse, right)
-
-
-def right_own_kernel(last, tiles_ref, high_ref, low_ref, out_ref):
-    out_ref[...] = right_rows(last, own_matrix(), tiles_ref, high_ref, low_ref)
+    return exact_dot(exact_dot(inverse, inverse, TN), right)
+
+
+def right_own_kernel(last, tiles_ref, high_ref, low_ref, out_ref, *gram_ref):
+    three = three_terms(rows_of(tiles_ref))
+    gram = gram_of(three)
+    if not last:
+        gram_ref[0][...] = gram
+    out_ref[...] = right_rows(last, own_matrix(), three, gram, high_ref, low_ref)
 
 
 def right_both_kernel(last, mine_ref, tiles_ref, high_ref, low_ref, out_ref):
     own = own_matrix()
     mine = mine_ref[...]
-    other = right_rows(last, 1 - own, tiles_ref, high_ref, low_ref)
+    three = three_terms(rows_of(tiles_ref))
+    other = right_rows(last, 1 - own, three, gram_of(three) if last else None, high_ref, low_ref)
     for copy in range(out_ref.shape[0]):
         out_ref[copy, own] = mine
         out_ref[copy, 1 - own] = other
 
 
 def right_terms(last, copies, tiles, high, low):
-    other = lax.ppermute(tiles, "core", [(0, 1), (1, 0)])
-    shared = dict(out_specs=WHOLE, compiler_params=params(24))
-    mine = pl.pallas_call(
+    other = swapped(tiles)
+    shapes = [jax.ShapeDtypeStruct((RANK, LANES), F32)] + [jax.ShapeDtypeStruct((RANK, RANK), F32)] * (not last)
+    mine, *gram = pl.pallas_call(
         functools.partial(right_own_kernel, last),
         in_specs=[WHOLE] * 3,
-        out_shape=jax.ShapeDtypeStruct((RANK, LANES), F32),
+        out_specs=[WHOLE] * len(shapes),
+        out_shape=shapes,
+        compiler_params=params(24),
         name="right_own",
-        **shared,
     )(tiles, in_vmem(high), in_vmem(low))
     both = pl.pallas_call(
         functools.partial(right_both_kernel, last),
         in_specs=[WHOLE] * 4,
+        out_specs=WHOLE,
         out_shape=jax.ShapeDtypeStruct((copies, 2, RANK, LANES), F32),
+        compiler_params=params(24),
         name="right_both",
-        **shared,
     )(mine, other, in_vmem(high), in_vmem(low))
-    return both, other
+    return both, other, gram
 
 
 def total(parts_ref, m):
     return sum(parts_ref[r, m] for r in range(parts_ref.shape[0]))
 
 
-def left_kernel(mine, parts_ref, high_ref, low_ref, term_ref):
-    m = own_matrix() if mine else 1 - own_matrix()
+def left_rows(m, parts_ref, high_ref, low_ref, term_ref):
     part = rows_at(m)
     f_high, f_low = split(total(parts_ref, m))
     both = jnp.concatenate([f_high, f_low], axis=0)
@@ -249,15 +263,13 @@
             term_ref[first // LANES + b] = terms[:, b * LANES : (b + 1) * LANES]
 
 
-def left_terms(mine, parts, high, low):
-    return pl.pallas_call(
-        functools.partial(left_kernel, mine),
-        in_specs=[WHOLE] * 3,
-        out_specs=WHOLE,
-        out_shape=jax.ShapeDtypeStruct((high.shape[1] // LANES, RANK, LANES), F32),
-        compiler_params=params(24),
-        name="left_own" if mine else "left_other",
-    )(parts, in_vmem(high), in_vmem(low))
+def left_other_kernel(parts_ref, high_ref, low_ref, term_ref):
+    left_rows(1 - own_matrix(), parts_ref, high_ref, low_ref, term_ref)
+
+
+def left_own_kernel(parts_ref, gram_ref, high_ref, low_ref, term_ref, inverse_ref):
+    inverse_ref[...] = inverse_of_factor(gram_ref[...])
+    left_rows(own_matrix(), parts_ref, high_ref, low_ref, term_ref)
 
 
 def add_kernel(x_ref, y_ref, out_ref):
@@ -275,33 +287,51 @@
     )(x, y)
 
 
-def chip_terms(parts, high, low):
-    sent = lax.ppermute(left_terms(False, parts, high, low), "core", [(0, 1), (1, 0)])
-    return added(sent, left_terms(True, parts, high, low))
-
-
-def spread_kernel(parts_ref, out_ref):
+def chip_terms(parts, gram, high, low):
+    tiles = jax.ShapeDtypeStruct((high.shape[1] // LANES, RANK, LANES), F32)
+    high, low = in_vmem(high), in_vmem(low)
+    send = pl.pallas_call(
+        left_other_kernel,
+        in_specs=[WHOLE] * 3,
+        out_specs=WHOLE,
+        out_shape=tiles,
+        compiler_params=params(24),
+        name="left_other",
+    )(parts, high, low)
+    sent = swapped(send)
+    keep, inverse = pl.pallas_call(
+        left_own_kernel,
+        in_specs=[WHOLE] * 4,
+        out_specs=[WHOLE] * 2,
+        out_shape=[tiles, jax.ShapeDtypeStruct((RANK, RANK), F32)],
+        compiler_params=params(24),
+        name="left_own",
+    )(parts, gram, high, low)
+    return added(sent, keep), inverse
+
+
+def spread_kernel(parts_ref, *rest):
+    out_ref = rest[-1]
     total = parts_ref[0]
     for r in range(1, parts_ref.shape[0]):
         total = total + parts_ref[r]
+    if len(rest) > 1:
+        total = exact_dot(rest[0][...], total)
     for r in range(out_ref.shape[0]):
         out_ref[r] = total
 
 
-def spread_sum(parts, copies):
-    return pl.pallas_call(
+def sum_own(tiles, *inverse):
+    parts = lax.all_to_all(tiles, ("dp", "x"), 0, 0)
+    spread = pl.pallas_call(
         spread_kernel,
-        in_specs=[WHOLE],
+        in_specs=[WHOLE] * (1 + len(inverse)),
         out_specs=WHOLE,
-        out_shape=jax.ShapeDtypeStruct((copies,) + parts.shape[1:], F32),
+        out_shape=jax.ShapeDtypeStruct(tiles.shape, F32),
         compiler_params=params(8),
         name="spread",
-    )(parts)
-
-
-def sum_own(tiles):
-    parts = lax.all_to_all(tiles, ("dp", "x"), 0, 0)
-    return lax.all_to_all(spread_sum(parts, tiles.shape[0]), ("dp", "x"), 0, 0)
+    )(parts, *inverse)
+    return lax.all_to_all(spread, ("dp", "x"), 0, 0)
 
 
 def mean_columns(weights, tiles):
@@ -312,7 +342,7 @@
     return dot(left, right, TN)
 
 
-def final_kernel(replicas, block, parts_ref, mine_ref, other_ref, high_ref, low_ref, decoded_ref, error_ref, held, sems):
+def final_kernel(replicas, block, parts_ref, mine_ref, other_ref, high_ref, low_ref, decoded_ref, error_ref, held, decoded, sems):
     weights = [total(parts_ref, m) / replicas for m in range(2)]
     own = own_matrix()
 
@@ -321,18 +351,21 @@
         return mean_columns(weights[m], jnp.where(own == m, mine, other))
 
     copies = []
-    for i in range(high_ref.shape[1] // block):
+    count = high_ref.shape[1] // block
+    for i in range(count):
         columns = pl.ds(i * block, block)
         for m in range(2):
             part = pl.ds(m * LANES, LANES)
             updates = high_ref[part, columns].astype(F32) + low_ref[part, columns].astype(F32)
             held[m, 0, columns] = (updates - mean(m, i * block // LANES, block // LANES)).astype(BF16).T
-        copy = pltpu.make_async_copy(held.at[:, :, columns], error_ref.at[:, :, columns], sems.at[i])
-        copy.start()
-        copies.append(copy)
-    count = decoded_ref.shape[1] // LANES
-    for m in range(2):
-        decoded_ref[m] = mean(m, lax.axis_index("dp") * count, count).T.astype(BF16)
+        copies.append(pltpu.make_async_copy(held.at[:, :, columns], error_ref.at[:, :, columns], sems.at[i]))
+        copies[-1].start()
+        if i == 0:
+            tiles = decoded.shape[1] // LANES
+            for m in range(2):
+                decoded[m] = mean(m, lax.axis_index("dp") * tiles, tiles).T.astype(BF16)
+            copies.append(pltpu.make_async_copy(decoded, decoded_ref, sems.at[count]))
+            copies[-1].start()
     for copy in copies:
         copy.wait()
 
@@ -343,14 +376,15 @@
     return pl.pallas_call(
         functools.partial(final_kernel, replicas, block),
         in_specs=[WHOLE] * 5,
-        out_specs=[WHOLE, pl.BlockSpec(memory_space=pl.ANY)],
+        out_specs=[pl.BlockSpec(memory_space=pl.ANY)] * 2,
         out_shape=[
             jax.ShapeDtypeStruct((2, d // replicas, LANES), BF16),
             jax.ShapeDtypeStruct((2, 1, d, LANES), BF16),
         ],
         scratch_shapes=[
             pltpu.VMEM((2, 1, d, LANES), BF16),
-            pltpu.SemaphoreType.DMA((d // block,)),
+            pltpu.VMEM((2, d // replicas, LANES), BF16),
+            pltpu.SemaphoreType.DMA((1 + d // block,)),
         ],
         compiler_params=params(24),
         name="final",
@@ -360,13 +394,10 @@
 def local(activations, output_grads, error_feedback, warm_start):
     replicas = lax.axis_size("dp")
     high, low, term = make_updates(activations, output_grads, error_feedback, jnp.swapaxes(warm_start, 1, 2))
-    mine = sum_own(term)
-    terms, other = right_terms(False, replicas, mine, high, low)
-    parts = lax.all_to_all(terms, "dp", 0, 0)
-    mine = sum_own(chip_terms(parts, high, low))
-    terms, other = right_terms(True, replicas, mine, high, low)
-    parts = lax.all_to_all(terms, "dp", 0, 0)
-    return tuple(final_outputs(replicas, parts, mine, other, high, low))
+    terms, _, (gram,) = right_terms(False, replicas, sum_own(term), high, low)
+    mine = sum_own(*chip_terms(lax.all_to_all(terms, "dp", 0, 0), gram, high, low))
+    terms, other, _ = right_terms(True, replicas, mine, high, low)
+    return tuple(final_outputs(replicas, lax.all_to_all(terms, "dp", 0, 0), mine, other, high, low))
 
 
 def solution(mesh):

time: 115 us -> 115 us (level)
  transfers between devices with their start and end apart: 4 -> 4, of which waited for: 1 -> 2; matrix products, arithmetic and copies ran while one was open for 0% -> 0% of each run, Pallas kernels for 5% -> 5%
where the time goes in v5:
time: 115 us; the launch traced here: 114 us
  blocking collectives  90.9 us (79%)
  Pallas kernels  21.6 us (19%)
    all_to_all x2, blocking collectives, sum_own(): parts = lax.all_to_all(tiles, ('dp', 'x'), 0, 0)  38.4 us
    all_to_all x2, blocking collectives, sum_own(): return lax.all_to_all(spread, ('dp', 'x'), 0, 0)  30.5 us
    all_to_all x2, blocking collectives, local(): lax.all_to_all(terms, 'dp', 0, 0)  21.9 us
    pallas_call x1, Pallas kernels, make_updates(): pl.pallas_call(functools.partial(updates_kernel, chunk, head), in_specs=[...  8.81 us
    pallas_call x1, Pallas kernels, final_outputs(): pl.pallas_call(functools.partial(final_kernel, replicas, block), in_specs...  3.32 us
    pallas_call x2, Pallas kernels, right_terms(): pl.pallas_call(functools.partial(right_own_kernel, last), in_specs=[WHOLE...  3.06 us
    pallas_call x2, Pallas kernels, right_terms(): pl.pallas_call(functools.partial(right_both_kernel, last), in_specs=[WHOL...  3.01 us
  transfers between devices with their start and end apart: 4, of which 2 were waited for; matrix products, arithmetic and copies ran while one was open for 0% of the time, Pallas kernels for 5%

profile of v5, /device:TPU:0, one launch (start us, length us, event | category | flops | bytes accessed | tf_op | source)
XLA Modules:
  0.0 114.4 jit_solution(6058171774077560738)
XLA Ops:
  0.6 8.8 %updates.1 = (bf16[256,8192]{1,0:T(8,128)(2,1)S(1)}, bf16[256,8192]{1,0:T(8,128)(2,1)S(1)}, f32[64,8,128]{2,1,0:T(8,128)S(1)}, f32[64,8,128]{2,1,0:T(8,128)S(1)}...) custom-call(bf16[1024,8192]{1,0:T(8,128)(2,1)} %act_ref.1, ...), custom_call_target="tpu_custom_call" | custom-call | tf_op jit(solution)/shard_map/updates/pallas_call | solution.py:147
  9.4 0.1 collective-permute-start
  9.5 1.5 %updates_tail.1 = (bf16[256,8192]{1,0:T(8,128)(2,1)S(1)}, bf16[256,8192]{1,0:T(8,128)(2,1)S(1)}, f32[64,8,128]{2,1,0:T(8,128)S(1)}) custom-call(bf16[1024,2048]{1,0:T(8,128)(2,1)S(1)} %get-tuple-element.17.act_ref, bf16[2,1,2048,128]{3,2,1,0:T(8,128)(2,1)S(1)} %get-tuple-element.18.error_ref, ...), custom_call_target="tpu_custom_call", output_to_operand_aliasing={{0}: (4, {}), {1}: (5, {})} | custom-call | tf_op jit(solution)/shard_map/updates_tail/pallas_call | solution.py:164
  11.0 0.0 collective-permute-done.x_ref
  11.1 22.5 %all_to_all.30.parts_ref = f32[64,8,128]{2,1,0:T(8,128)S(1)} all-to-all(f32[64,8,128]{2,1,0:T(8,128)S(1)} %add.2), channel_id=1, replica_groups=mesh['dp'=16,'x'=4,'core'=2] {'dp','x'}, dimensions={0} | all-to-all | bytes 524288 | tf_op jit(solution)/shard_map/all_to_all | solution.py:325
  33.6 0.1 spread.2
  33.7 15.3 %all_to_all.31.tiles_ref = f32[64,8,128]{2,1,0:T(8,128)S(1)} all-to-all(f32[64,8,128]{2,1,0:T(8,128)S(1)} %spread.2), channel_id=1, replica_groups=mesh['dp'=16,'x'=4,'core'=2] {'dp','x'}, dimensions={0} | all-to-all | bytes 524288 | tf_op jit(solution)/shard_map/all_to_all | solution.py:334
  49.0 0.0 collective-permute-start.1
  49.0 1.3 %right_own.2 = (f32[8,128]{1,0:T(8,128)S(1)}, f32[8,8]{1,0:T(8,128)S(1)}) custom-call(f32[64,8,128]{2,1,0:T(8,128)S(1)} %all_to_all.31.tiles_ref, bf16[256,8192]{1,0:T(8,128)(2,1)S(1)} %get-tuple-element.24.high_ref, bf16[256,8192]{1,0:T(8,128)(2,1)S(1)} %get-tuple-element.25.low_ref), custom_call_target="tpu_custom_call" | custom-call | tf_op jit(solution)/shard_map/right_own/pallas_call | solution.py:231
  50.3 0.2 collective-permute-done.1.tiles_ref
  50.5 1.2 %right_both.2 = f32[16,2,8,128]{3,2,1,0:T(8,128)S(1)} custom-call(f32[8,128]{1,0:T(8,128)S(1)} %get-tuple-element.26.mine_ref, f32[64,8,128]{2,1,0:T(8,128)S(1)} %collective-permute-done.1.tiles_ref, bf16[256,8192]{1,0:T(8,128)(2,1)S(1)} %get-tuple-element.24.high_ref, bf16[256,8192]{1,0:T(8,128)(2,1)S(1)} %get-tuple-element.25.low_ref), custom_call_target="tpu_custom_call" | custom-call | tf_op jit(solution)/shard_map/right_both/pallas_call | solution.py:239
  51.8 10.9 %all_to_all.32.parts_ref = f32[16,2,8,128]{3,2,1,0:T(8,128)S(1)} all-to-all(f32[16,2,8,128]{3,2,1,0:T(8,128)S(1)} %right_both.2), channel_id=1, replica_groups=mesh['dp'=16,'x'=4,'core'=2] {'dp'}, dimensions={0} | all-to-all | bytes 262144 | tf_op jit(solution)/shard_map/all_to_all | solution.py:398
  62.7 0.7 left_other.1
  63.3 0.1 collective-permute-start.2
  63.4 0.9 left_own.1
  64.3 0.6 collective-permute-done.2.x_ref
  65.0 15.9 %all_to_all.33.parts_ref = f32[64,8,128]{2,1,0:T(8,128)S(1)} all-to-all(f32[64,8,128]{2,1,0:T(8,128)S(1)} %add.3), channel_id=1, replica_groups=mesh['dp'=16,'x'=4,'core'=2] {'dp','x'}, dimensions={0} | all-to-all | bytes 524288 | tf_op jit(solution)/shard_map/all_to_all | solution.py:325
  80.9 0.2 spread.3
  81.1 15.3 %all_to_all.34.tiles_ref.mine_ref = f32[64,8,128]{2,1,0:T(8,128)S(1)} all-to-all(f32[64,8,128]{2,1,0:T(8,128)S(1)} %spread.3), channel_id=1, replica_groups=mesh['dp'=16,'x'=4,'core'=2] {'dp','x'}, dimensions={0} | all-to-all | bytes 524288 | tf_op jit(solution)/shard_map/all_to_all | solution.py:334
  96.3 0.0 collective-permute-start.3
  96.3 1.7 %right_own.3.mine_ref = f32[8,128]{1,0:T(8,128)S(1)} custom-call(f32[64,8,128]{2,1,0:T(8,128)S(1)} %all_to_all.34.tiles_ref.mine_ref, bf16[256,8192]{1,0:T(8,128)(2,1)S(1)} %get-tuple-element.24.high_ref, bf16[256,8192]{1,0:T(8,128)(2,1)S(1)} %get-tuple-element.25.low_ref), custom_call_target="tpu_custom_call" | custom-call | tf_op jit(solution)/shard_map/right_own/pallas_call | solution.py:231
  98.1 0.0 collective-permute-done.3.tiles_ref.other_ref
  98.1 1.8 %right_both.3 = f32[16,2,8,128]{3,2,1,0:T(8,128)S(1)} custom-call(f32[8,128]{1,0:T(8,128)S(1)} %right_own.3.mine_ref, f32[64,8,128]{2,1,0:T(8,128)S(1)} %collective-permute-done.3.tiles_ref.other_ref, bf16[256,8192]{1,0:T(8,128)(2,1)S(1)} %get-tuple-element.24.high_ref, bf16[256,8192]{1,0:T(8,128)(2,1)S(1)} %get-tuple-element.25.low_ref), custom_call_target="tpu_custom_call" | custom-call | tf_op jit(solution)/shard_map/right_both/pallas_call | solution.py:239
  99.9 11.0 %all_to_all.35.parts_ref = f32[16,2,8,128]{3,2,1,0:T(8,128)S(1)} all-to-all(f32[16,2,8,128]{3,2,1,0:T(8,128)S(1)} %right_both.3), channel_id=1, replica_groups=mesh['dp'=16,'x'=4,'core'=2] {'dp'}, dimensions={0} | all-to-all | bytes 262144 | tf_op jit(solution)/shard_map/all_to_all | solution.py:400
  110.9 3.3 %final.1 = (bf16[2,512,128]{2,1,0:T(8,128)(2,1)}, bf16[2,1,8192,128]{3,2,1,0:T(8,128)(2,1)}) custom-call(f32[16,2,8,128]{3,2,1,0:T(8,128)S(1)} %all_to_all.35.parts_ref, f32[64,8,128]{2,1,0:T(8,128)S(1)} %all_to_all.34.tiles_ref.mine_ref, f32[64,8,128]{2,1,0:T(8,128)S(1)} %collective-permute-done.3.tiles_ref.other_ref, ...), custom_call_target="tpu_custom_call" | custom-call | tf_op jit(solution)/shard_map/final/pallas_call | solution.py:376
  (2 shorter events, 0.1 us)
Async XLA Ops:
  9.4 1.6 %collective-permute-start = (f32[64,8,128]{2,1,0:T(8,128)S(1)}, f32[64,8,128]{2,1,0:T(8,128)S(1)}, u32[]{:S(2)}, u32[]{:S(2)}) collective-permute-start(f32[64,8,128]{2,1,0:T(8,128)S(1)} %get-tuple-element.16), channel_id=1, source_target_pairs={{0,1},{1,0},{2,3},{3,2},{4,5},{5,4},{6,7},{7,6},{8,9},{9,8},{10,11... | collective-permute-start | bytes 786440 | tf_op jit(solution)/shard_map/ppermute | solution.py:60
  49.0 1.5 %collective-permute-start.1 = (f32[64,8,128]{2,1,0:T(8,128)S(1)}, f32[64,8,128]{2,1,0:T(8,128)S(1)}, u32[]{:S(2)}, u32[]{:S(2)}) collective-permute-start(f32[64,8,128]{2,1,0:T(8,128)S(1)} %all_to_all.31.tiles_ref), channel_id=1, source_target_pairs={{0,1},{1,0},{2,3},{3,2},{4,5},{5,4},{6,7},{7,6},{8,9},{9,8},{10,11... | collective-permute-start | bytes 786440 | tf_op jit(solution)/shard_map/ppermute | solution.py:60
  63.3 1.6 %collective-permute-start.2 = (f32[64,8,128]{2,1,0:T(8,128)S(1)}, f32[64,8,128]{2,1,0:T(8,128)S(1)}, u32[]{:S(2)}, u32[]{:S(2)}) collective-permute-start(f32[64,8,128]{2,1,0:T(8,128)S(1)} %left_other.1), channel_id=1, source_target_pairs={{0,1},{1,0},{2,3},{3,2},{4,5},{5,4},{6,7},{7,6},{8,9},{9,8},{10,11... | collective-permute-start | bytes 786440 | tf_op jit(solution)/shard_map/ppermute | solution.py:60
  96.3 1.7 %collective-permute-start.3 = (f32[64,8,128]{2,1,0:T(8,128)S(1)}, f32[64,8,128]{2,1,0:T(8,128)S(1)}, u32[]{:S(2)}, u32[]{:S(2)}) collective-permute-start(f32[64,8,128]{2,1,0:T(8,128)S(1)} %all_to_all.34.tiles_ref.mine_ref), channel_id=1, source_target_pairs={{0,1},{1,0},{2,3},{3,2},{4,5},{5,4},{6,7},{7,6},{8,9},{9,8},{10,11... | collective-permute-start | bytes 786440 | tf_op jit(solution)/shard_map/ppermute | solution.py:60

commit v6 on v5

--- a/solution.py
+++ b/solution.py
@@ -102,8 +102,11 @@
     step = min(STEP, chunk)
     for i, pair in enumerate(copies):
         act_at, error_at, shift = places[i]
-        for copy in pair:
-            copy.wait()
+        pair[0].wait()
+        if i >= head:
+            every = pl.ds(i * chunk - shift, chunk)
+            ahead = [dot(warm[m], error_at[m, 0, every], NT) for m in range(2)]
+        pair[1].wait()
         for first in range(i * chunk, (i + 1) * chunk, step):
             here = pl.ds(first - shift, step)
             if i < head:
@@ -114,7 +117,7 @@
                 moved = [dot(warm[m], turned[m]) for m in range(2)]
             else:
                 left = dot(taken, act_at[:, here])
-                moved = [dot(warm[m], error_at[m, 0, here], NT) for m in range(2)]
+                moved = [x[:, first - i * chunk : first - i * chunk + step] for x in ahead]
             terms = folded(left) + jnp.concatenate([folded(x) for x in moved], axis=0)
             key, value = terms[:RANK], terms[RANK:]
             keep, send = jnp.where(first_core, key, value), jnp.where(first_core, value, key)
@@ -198,53 +201,58 @@
     return sum(gram[:, i * RANK : (i + 1) * RANK] for i in range(3))
 
 
-def right_rows(last, m, three, gram, high_ref, low_ref):
+def right_rows(m, three, high_ref, low_ref):
     part = rows_at(m)
-    right = folded(dot(three[: 2 * RANK], high_ref[part, :], NT)) + dot(three[:RANK], low_ref[part, :], NT)
-    if not last:
-        return right
+    return folded(dot(three[: 2 * RANK], high_ref[part, :], NT)) + dot(three[:RANK], low_ref[part, :], NT)
+
+
+def inverse_of_gram(gram):
     inverse = inverse_of_factor(gram)
-    return exact_dot(exact_dot(inverse, inverse, TN), right)
-
-
-def right_own_kernel(last, tiles_ref, high_ref, low_ref, out_ref, *gram_ref):
+    return exact_dot(inverse, inverse, TN)
+
+
+def right_own_kernel(last, tiles_ref, high_ref, low_ref, out_ref, norm_ref):
     three = three_terms(rows_of(tiles_ref))
     gram = gram_of(three)
-    if not last:
-        gram_ref[0][...] = gram
-    out_ref[...] = right_rows(last, own_matrix(), three, gram, high_ref, low_ref)
-
-
-def right_both_kernel(last, mine_ref, tiles_ref, high_ref, low_ref, out_ref):
+    out_ref[...] = right_rows(own_matrix(), three, high_ref, low_ref)
+    norm_ref[...] = inverse_of_gram(gram) if last else gram
+
+
+def right_both_kernel(last, mine_ref, tiles_ref, high_ref, low_ref, out_ref, *norm_ref):
     own = own_matrix()
     mine = mine_ref[...]
     three = three_terms(rows_of(tiles_ref))
-    other = right_rows(last, 1 - own, three, gram_of(three) if last else None, high_ref, low_ref)
+    if last:
+        gram = gram_of(three)
+    other = right_rows(1 - own, three, high_ref, low_ref)
     for copy in range(out_ref.shape[0]):
         out_ref[copy, own] = mine
         out_ref[copy, 1 - own] = other
+    if last:
+        norm_ref[0][...] = inverse_of_gram(gram)
 
 
 def right_terms(last, copies, tiles, high, low):
     other = swapped(tiles)
-    shapes = [jax.ShapeDtypeStruct((RANK, LANES), F32)] + [jax.ShapeDtypeStruct((RANK, RANK), F32)] * (not last)
-    mine, *gram = pl.pallas_call(
+    norm = jax.ShapeDtypeStruct((RANK, RANK), F32)
+    mine, own_norm = pl.pallas_call(
         functools.partial(right_own_kernel, last),
         in_specs=[WHOLE] * 3,
+        out_specs=[WHOLE] * 2,
+        out_shape=[jax.ShapeDtypeStruct((RANK, LANES), F32), norm],
+        compiler_params=params(24),
+        name="right_own",
+    )(tiles, in_vmem(high), in_vmem(low))
+    shapes = [jax.ShapeDtypeStruct((copies, 2, RANK, LANES), F32)] + [norm] * last
+    both, *other_norm = pl.pallas_call(
+        functools.partial(right_both_kernel, last),
+        in_specs=[WHOLE] * 4,
         out_specs=[WHOLE] * len(shapes),
         out_shape=shapes,
         compiler_params=params(24),
-        name="right_own",
-    )(tiles, in_vmem(high), in_vmem(low))
-    both = pl.pallas_call(
-        functools.partial(right_both_kernel, last),
-        in_specs=[WHOLE] * 4,
-        out_specs=WHOLE,
-        out_shape=jax.ShapeDtypeStruct((copies, 2, RANK, LANES), F32),
-        compiler_params=params(24),
         name="right_both",
     )(mine, other, in_vmem(high), in_vmem(low))
-    return both, other, gram
+    return both, other, [own_norm] + other_norm
 
 
 def total(parts_ref, m):
@@ -342,22 +350,25 @@
     return dot(left, right, TN)
 
 
-def final_kernel(replicas, block, parts_ref, mine_ref, other_ref, high_ref, low_ref, decoded_ref, error_ref, held, decoded, sems):
-    weights = [total(parts_ref, m) / replicas for m in range(2)]
+def final_kernel(replicas, block, parts_ref, mine_ref, other_ref, own_norm, other_norm, high_ref, low_ref, decoded_ref, error_ref, held, decoded, sems):
     own = own_matrix()
+    norms = [jnp.where(own == m, own_norm[...], other_norm[...]) for m in range(2)]
+    weights = [exact_dot(norms[m], total(parts_ref, m)) / replicas for m in range(2)]
 
     def mean(m, first, count):
         mine, other = (rows_of(ref, first, count) for ref in (mine_ref, other_ref))
         return mean_columns(weights[m], jnp.where(own == m, mine, other))
 
     copies = []
-    count = high_ref.shape[1] // block
-    for i in range(count):
-        columns = pl.ds(i * block, block)
+    d = high_ref.shape[1]
+    starts = list(range(0, d, block)) + [d - block // 2]
+    count = len(starts)
+    for i, (first, end) in enumerate(zip(starts, starts[1:] + [d])):
+        columns = pl.ds(first, end - first)
         for m in range(2):
             part = pl.ds(m * LANES, LANES)
             updates = high_ref[part, columns].astype(F32) + low_ref[part, columns].astype(F32)
-            held[m, 0, columns] = (updates - mean(m, i * block // LANES, block // LANES)).astype(BF16).T
+            held[m, 0, columns] = (updates - mean(m, first // LANES, (end - first) // LANES)).astype(BF16).T
         copies.append(pltpu.make_async_copy(held.at[:, :, columns], error_ref.at[:, :, columns], sems.at[i]))
         copies[-1].start()
         if i == 0:
@@ -370,12 +381,12 @@
         copy.wait()
 
 
-def final_outputs(replicas, parts, mine, other, high, low):
+def final_outputs(replicas, parts, mine, other, norms, high, low):
     d = high.shape[1]
     block = min(1024, d)
     return pl.pallas_call(
         functools.partial(final_kernel, replicas, block),
-        in_specs=[WHOLE] * 5,
+        in_specs=[WHOLE] * 7,
         out_specs=[pl.BlockSpec(memory_space=pl.ANY)] * 2,
         out_shape=[
             jax.ShapeDtypeStruct((2, d // replicas, LANES), BF16),
@@ -384,11 +395,11 @@
         scratch_shapes=[
             pltpu.VMEM((2, 1, d, LANES), BF16),
             pltpu.VMEM((2, d // replicas, LANES), BF16),
-            pltpu.SemaphoreType.DMA((1 + d // block,)),
+            pltpu.SemaphoreType.DMA((2 + d // block,)),
         ],
         compiler_params=params(24),
         name="final",
-    )(parts, mine, other, in_vmem(high), in_vmem(low))
+    )(parts, mine, other, *norms, in_vmem(high), in_vmem(low))
 
 
 def local(activations, output_grads, error_feedback, warm_start):
@@ -396,8 +407,8 @@
     high, low, term = make_updates(activations, output_grads, error_feedback, jnp.swapaxes(warm_start, 1, 2))
     terms, _, (gram,) = right_terms(False, replicas, sum_own(term), high, low)
     mine = sum_own(*chip_terms(lax.all_to_all(terms, "dp", 0, 0), gram, high, low))
-    terms, other, _ = right_terms(True, replicas, mine, high, low)
-    return tuple(final_outputs(replicas, lax.all_to_all(terms, "dp", 0, 0), mine, other, high, low))
+    terms, other, norms = right_terms(True, replicas, mine, high, low)
+    return tuple(final_outputs(replicas, lax.all_to_all(terms, "dp", 0, 0), mine, other, norms, high, low))
 
 
 def solution(mesh):

time: 115 us -> 115 us (level)
  no operation moved by 1% of the time
where the time goes in v6:
time: 115 us
  blocking collectives  90.9 us (79%)
  Pallas kernels  21.8 us (19%)
    all_to_all x2, blocking collectives, sum_own(): parts = lax.all_to_all(tiles, ('dp', 'x'), 0, 0)  38.4 us
    all_to_all x2, blocking collectives, sum_own(): return lax.all_to_all(spread, ('dp', 'x'), 0, 0)  30.5 us
    all_to_all x2, blocking collectives, local(): lax.all_to_all(terms, 'dp', 0, 0)  21.9 us
    pallas_call x1, Pallas kernels, make_updates(): pl.pallas_call(functools.partial(updates_kernel, chunk, head), in_specs=[...  9.09 us
    pallas_call x1, Pallas kernels, final_outputs(): pl.pallas_call(functools.partial(final_kernel, replicas, block), in_specs...  3.52 us
    pallas_call x2, Pallas kernels, right_terms(): pl.pallas_call(functools.partial(right_own_kernel, last), in_specs=[WHOLE...  2.92 us
    pallas_call x2, Pallas kernels, right_terms(): pl.pallas_call(functools.partial(right_both_kernel, last), in_specs=[WHOL...  2.84 us
  transfers between devices with their start and end apart: 4, of which 2 were waited for; matrix products, arithmetic and copies ran while one was open for 0% of the time, Pallas kernels for 5%

profile of v6, /device:TPU:0, one launch (start us, length us, event | category | flops | bytes accessed | tf_op | source)
XLA Modules:
  0.0 114.7 jit_solution(9024632273932974508)
XLA Ops:
  0.6 9.1 %updates.1 = (bf16[256,8192]{1,0:T(8,128)(2,1)S(1)}, bf16[256,8192]{1,0:T(8,128)(2,1)S(1)}, f32[64,8,128]{2,1,0:T(8,128)S(1)}, f32[64,8,128]{2,1,0:T(8,128)S(1)}...) custom-call(bf16[1024,8192]{1,0:T(8,128)(2,1)} %act_ref.1, ...), custom_call_target="tpu_custom_call" | custom-call | tf_op jit(solution)/shard_map/updates/pallas_call | solution.py:150
  9.7 0.1 collective-permute-start
  9.8 1.5 %updates_tail.1 = (bf16[256,8192]{1,0:T(8,128)(2,1)S(1)}, bf16[256,8192]{1,0:T(8,128)(2,1)S(1)}, f32[64,8,128]{2,1,0:T(8,128)S(1)}) custom-call(bf16[1024,2048]{1,0:T(8,128)(2,1)S(1)} %get-tuple-element.21.act_ref, bf16[2,1,2048,128]{3,2,1,0:T(8,128)(2,1)S(1)} %get-tuple-element.22.error_ref, ...), custom_call_target="tpu_custom_call", output_to_operand_aliasing={{0}: (4, {}), {1}: (5, {})} | custom-call | tf_op jit(solution)/shard_map/updates_tail/pallas_call | solution.py:167
  11.3 0.0 collective-permute-done.x_ref
  11.4 22.5 %all_to_all.30.parts_ref = f32[64,8,128]{2,1,0:T(8,128)S(1)} all-to-all(f32[64,8,128]{2,1,0:T(8,128)S(1)} %add.2), channel_id=1, replica_groups=mesh['dp'=16,'x'=4,'core'=2] {'dp','x'}, dimensions={0} | all-to-all | bytes 524288 | tf_op jit(solution)/shard_map/all_to_all | solution.py:333
  33.9 0.1 spread.2
  34.0 15.3 %all_to_all.31.tiles_ref = f32[64,8,128]{2,1,0:T(8,128)S(1)} all-to-all(f32[64,8,128]{2,1,0:T(8,128)S(1)} %spread.2), channel_id=1, replica_groups=mesh['dp'=16,'x'=4,'core'=2] {'dp','x'}, dimensions={0} | all-to-all | bytes 524288 | tf_op jit(solution)/shard_map/all_to_all | solution.py:342
  49.3 0.0 collective-permute-start.1
  49.3 1.3 %right_own.2 = (f32[8,128]{1,0:T(8,128)S(1)}, f32[8,8]{1,0:T(8,128)S(1)}) custom-call(f32[64,8,128]{2,1,0:T(8,128)S(1)} %all_to_all.31.tiles_ref, bf16[256,8192]{1,0:T(8,128)(2,1)S(1)} %get-tuple-element.28.high_ref, bf16[256,8192]{1,0:T(8,128)(2,1)S(1)} %get-tuple-element.29.low_ref), custom_call_target="tpu_custom_call" | custom-call | tf_op jit(solution)/shard_map/right_own/pallas_call | solution.py:238
  50.6 0.2 collective-permute-done.1.tiles_ref
  50.8 1.2 %right_both.2 = f32[16,2,8,128]{3,2,1,0:T(8,128)S(1)} custom-call(f32[8,128]{1,0:T(8,128)S(1)} %get-tuple-element.30.mine_ref, f32[64,8,128]{2,1,0:T(8,128)S(1)} %collective-permute-done.1.tiles_ref, bf16[256,8192]{1,0:T(8,128)(2,1)S(1)} %get-tuple-element.28.high_ref, bf16[256,8192]{1,0:T(8,128)(2,1)S(1)} %get-tuple-element.29.low_ref), custom_call_target="tpu_custom_call" | custom-call | tf_op jit(solution)/shard_map/right_both/pallas_call | solution.py:247
  52.0 10.9 %all_to_all.32.parts_ref = f32[16,2,8,128]{3,2,1,0:T(8,128)S(1)} all-to-all(f32[16,2,8,128]{3,2,1,0:T(8,128)S(1)} %right_both.2), channel_id=1, replica_groups=mesh['dp'=16,'x'=4,'core'=2] {'dp'}, dimensions={0} | all-to-all | bytes 262144 | tf_op jit(solution)/shard_map/all_to_all | solution.py:409
  62.9 0.7 left_other.1
  63.6 0.2 collective-permute-start.2
  63.8 0.9 left_own.1
  64.8 0.6 collective-permute-done.2.x_ref
  65.4 15.9 %all_to_all.33.parts_ref = f32[64,8,128]{2,1,0:T(8,128)S(1)} all-to-all(f32[64,8,128]{2,1,0:T(8,128)S(1)} %add.3), channel_id=1, replica_groups=mesh['dp'=16,'x'=4,'core'=2] {'dp','x'}, dimensions={0} | all-to-all | bytes 524288 | tf_op jit(solution)/shard_map/all_to_all | solution.py:333
  81.3 0.2 spread.3
  81.5 15.3 %all_to_all.34.tiles_ref.mine_ref = f32[64,8,128]{2,1,0:T(8,128)S(1)} all-to-all(f32[64,8,128]{2,1,0:T(8,128)S(1)} %spread.3), channel_id=1, replica_groups=mesh['dp'=16,'x'=4,'core'=2] {'dp','x'}, dimensions={0} | all-to-all | bytes 524288 | tf_op jit(solution)/shard_map/all_to_all | solution.py:342
  96.8 0.0 collective-permute-start.3
  96.8 1.6 %right_own.3 = (f32[8,128]{1,0:T(8,128)S(1)}, f32[8,8]{1,0:T(8,128)S(1)}) custom-call(f32[64,8,128]{2,1,0:T(8,128)S(1)} %all_to_all.34.tiles_ref.mine_ref, bf16[256,8192]{1,0:T(8,128)(2,1)S(1)} %get-tuple-element.28.high_ref, bf16[256,8192]{1,0:T(8,128)(2,1)S(1)} %get-tuple-element.29.low_ref), custom_call_target="tpu_custom_call" | custom-call | tf_op jit(solution)/shard_map/right_own/pallas_call | solution.py:238
  98.4 0.0 collective-permute-done.3.tiles_ref.other_ref
  98.4 1.6 %right_both.3 = (f32[16,2,8,128]{3,2,1,0:T(8,128)S(1)}, f32[8,8]{1,0:T(8,128)S(1)}) custom-call(f32[8,128]{1,0:T(8,128)S(1)} %get-tuple-element.34.mine_ref, f32[64,8,128]{2,1,0:T(8,128)S(1)} %collective-permute-done.3.tiles_ref.other_ref, bf16[256,8192]{1,0:T(8,128)(2,1)S(1)} %get-tuple-element.28.high_ref, bf16[256,8192]{1,0:T(8,128)(2,1)S(1)} %get-tuple-element.29.low_ref), custom_call_target="tpu_custom_call" | custom-call | tf_op jit(solution)/shard_map/right_both/pallas_call | solution.py:247
  100.0 11.0 %all_to_all.35.parts_ref = f32[16,2,8,128]{3,2,1,0:T(8,128)S(1)} all-to-all(f32[16,2,8,128]{3,2,1,0:T(8,128)S(1)} %get-tuple-element.35), channel_id=1, replica_groups=mesh['dp'=16,'x'=4,'core'=2] {'dp'}, dimensions={0} | all-to-all | bytes 262144 | tf_op jit(solution)/shard_map/all_to_all | solution.py:411
  111.0 3.5 %final.1 = (bf16[2,512,128]{2,1,0:T(8,128)(2,1)}, bf16[2,1,8192,128]{3,2,1,0:T(8,128)(2,1)}) custom-call(f32[16,2,8,128]{3,2,1,0:T(8,128)S(1)} %all_to_all.35.parts_ref, f32[64,8,128]{2,1,0:T(8,128)S(1)} %all_to_all.34.tiles_ref.mine_ref, f32[64,8,128]{2,1,0:T(8,128)S(1)} %collective-permute-done.3.tiles_ref.other_ref, ...), custom_call_target="tpu_custom_call" | custom-call | tf_op jit(solution)/shard_map/final/pallas_call | solution.py:387
  (2 shorter events, 0.1 us)
Async XLA Ops:
  9.7 1.6 %collective-permute-start = (f32[64,8,128]{2,1,0:T(8,128)S(1)}, f32[64,8,128]{2,1,0:T(8,128)S(1)}, u32[]{:S(2)}, u32[]{:S(2)}) collective-permute-start(f32[64,8,128]{2,1,0:T(8,128)S(1)} %get-tuple-element.20), channel_id=1, source_target_pairs={{0,1},{1,0},{2,3},{3,2},{4,5},{5,4},{6,7},{7,6},{8,9},{9,8},{10,11... | collective-permute-start | bytes 786440 | tf_op jit(solution)/shard_map/ppermute | solution.py:60
  49.3 1.5 %collective-permute-start.1 = (f32[64,8,128]{2,1,0:T(8,128)S(1)}, f32[64,8,128]{2,1,0:T(8,128)S(1)}, u32[]{:S(2)}, u32[]{:S(2)}) collective-permute-start(f32[64,8,128]{2,1,0:T(8,128)S(1)} %all_to_all.31.tiles_ref), channel_id=1, source_target_pairs={{0,1},{1,0},{2,3},{3,2},{4,5},{5,4},{6,7},{7,6},{8,9},{9,8},{10,11... | collective-permute-start | bytes 786440 | tf_op jit(solution)/shard_map/ppermute | solution.py:60
  63.6 1.8 %collective-permute-start.2 = (f32[64,8,128]{2,1,0:T(8,128)S(1)}, f32[64,8,128]{2,1,0:T(8,128)S(1)}, u32[]{:S(2)}, u32[]{:S(2)}) collective-permute-start(f32[64,8,128]{2,1,0:T(8,128)S(1)} %left_other.1), channel_id=1, source_target_pairs={{0,1},{1,0},{2,3},{3,2},{4,5},{5,4},{6,7},{7,6},{8,9},{9,8},{10,11... | collective-permute-start | bytes 786440 | tf_op jit(solution)/shard_map/ppermute | solution.py:60
  96.8 1.6 %collective-permute-start.3 = (f32[64,8,128]{2,1,0:T(8,128)S(1)}, f32[64,8,128]{2,1,0:T(8,128)S(1)}, u32[]{:S(2)}, u32[]{:S(2)}) collective-permute-start(f32[64,8,128]{2,1,0:T(8,128)S(1)} %all_to_all.34.tiles_ref.mine_ref), channel_id=1, source_target_pairs={{0,1},{1,0},{2,3},{3,2},{4,5},{5,4},{6,7},{7,6},{8,9},{9,8},{10,11... | collective-permute-start | bytes 786440 | tf_op jit(solution)/shard_map/ppermute | solution.py:60

commit v7 on v6

--- a/solution.py
+++ b/solution.py
@@ -83,8 +83,8 @@
         here = part if i < head else pl.ds((i - head) * chunk, chunk)
         act_at, error_at = (act, errors) if i < head else (tail_act, tail_errors)
         pair = [
-            pltpu.make_async_copy(error_ref.at[:, :, part], error_at.at[:, :, here], sems.at[2 * i + 2]),
-            pltpu.make_async_copy(act_ref.at[:, part], act_at.at[:, here], sems.at[2 * i + 3]),
+            pltpu.make_async_copy(act_ref.at[:, part], act_at.at[:, here], sems.at[2 * i + 2]),
+            pltpu.make_async_copy(error_ref.at[:, :, part], error_at.at[:, :, here], sems.at[2 * i + 3]),
         ]
         for copy in pair:
             copy.start()
@@ -102,11 +102,8 @@
     step = min(STEP, chunk)
     for i, pair in enumerate(copies):
         act_at, error_at, shift = places[i]
-        pair[0].wait()
-        if i >= head:
-            every = pl.ds(i * chunk - shift, chunk)
-            ahead = [dot(warm[m], error_at[m, 0, every], NT) for m in range(2)]
-        pair[1].wait()
+        for copy in pair:
+            copy.wait()
         for first in range(i * chunk, (i + 1) * chunk, step):
             here = pl.ds(first - shift, step)
             if i < head:
@@ -117,7 +114,7 @@
                 moved = [dot(warm[m], turned[m]) for m in range(2)]
             else:
                 left = dot(taken, act_at[:, here])
-                moved = [x[:, first - i * chunk : first - i * chunk + step] for x in ahead]
+                moved = [dot(warm[m], error_at[m, 0, here], NT) for m in range(2)]
             terms = folded(left) + jnp.concatenate([folded(x) for x in moved], axis=0)
             key, value = terms[:RANK], terms[RANK:]
             keep, send = jnp.where(first_core, key, value), jnp.where(first_core, value, key)
@@ -361,14 +358,13 @@
 
     copies = []
     d = high_ref.shape[1]
-    starts = list(range(0, d, block)) + [d - block // 2]
-    count = len(starts)
-    for i, (first, end) in enumerate(zip(starts, starts[1:] + [d])):
-        columns = pl.ds(first, end - first)
+    count = d // block
+    for i, first in enumerate(range(0, d, block)):
+        columns = pl.ds(first, block)
         for m in range(2):
             part = pl.ds(m * LANES, LANES)
             updates = high_ref[part, columns].astype(F32) + low_ref[part, columns].astype(F32)
-            held[m, 0, columns] = (updates - mean(m, first // LANES, (end - first) // LANES)).astype(BF16).T
+            held[m, 0, columns] = (updates - mean(m, first // LANES, block // LANES)).astype(BF16).T
         copies.append(pltpu.make_async_copy(held.at[:, :, columns], error_ref.at[:, :, columns], sems.at[i]))
         copies[-1].start()
         if i == 0:
@@ -395,7 +391,7 @@
         scratch_shapes=[
             pltpu.VMEM((2, 1, d, LANES), BF16),
             pltpu.VMEM((2, d // replicas, LANES), BF16),
-            pltpu.SemaphoreType.DMA((2 + d // block,)),
+            pltpu.SemaphoreType.DMA((1 + d // block,)),
         ],
         compiler_params=params(24),
         name="final",

time: 115 us -> 115 us (level)
  no operation moved by 1% of the time
where the time goes in v7:
time: 115 us; the launch traced here: 114 us
  blocking collectives  90.9 us (79%)
  Pallas kernels  21.4 us (19%)
    all_to_all x2, blocking collectives, sum_own(): parts = lax.all_to_all(tiles, ('dp', 'x'), 0, 0)  38.4 us
    all_to_all x2, blocking collectives, sum_own(): return lax.all_to_all(spread, ('dp', 'x'), 0, 0)  30.5 us
    all_to_all x2, blocking collectives, local(): lax.all_to_all(terms, 'dp', 0, 0)  21.9 us
    pallas_call x1, Pallas kernels, make_updates(): pl.pallas_call(functools.partial(updates_kernel, chunk, head), in_specs=[...  8.73 us
    pallas_call x1, Pallas kernels, final_outputs(): pl.pallas_call(functools.partial(final_kernel, replicas, block), in_specs...  3.51 us
    pallas_call x2, Pallas kernels, right_terms(): pl.pallas_call(functools.partial(right_own_kernel, last), in_specs=[WHOLE...  2.92 us
    pallas_call x2, Pallas kernels, right_terms(): pl.pallas_call(functools.partial(right_both_kernel, last), in_specs=[WHOL...  2.84 us
  transfers between devices with their start and end apart: 4, of which 2 were waited for; matrix products, arithmetic and copies ran while one was open for 0% of the time, Pallas kernels for 5%

profile of v7, /device:TPU:0, one launch (start us, length us, event | category | flops | bytes accessed | tf_op | source)
XLA Modules:
  0.0 114.2 jit_solution(3326408453294319264)
XLA Ops:
  0.6 8.7 %updates.1 = (bf16[256,8192]{1,0:T(8,128)(2,1)S(1)}, bf16[256,8192]{1,0:T(8,128)(2,1)S(1)}, f32[64,8,128]{2,1,0:T(8,128)S(1)}, f32[64,8,128]{2,1,0:T(8,128)S(1)}...) custom-call(bf16[1024,8192]{1,0:T(8,128)(2,1)} %act_ref.1, ...), custom_call_target="tpu_custom_call" | custom-call | tf_op jit(solution)/shard_map/updates/pallas_call | solution.py:147
  9.4 0.1 collective-permute-start
  9.5 1.5 %updates_tail.1 = (bf16[256,8192]{1,0:T(8,128)(2,1)S(1)}, bf16[256,8192]{1,0:T(8,128)(2,1)S(1)}, f32[64,8,128]{2,1,0:T(8,128)S(1)}) custom-call(bf16[1024,2048]{1,0:T(8,128)(2,1)S(1)} %get-tuple-element.21.act_ref, bf16[2,1,2048,128]{3,2,1,0:T(8,128)(2,1)S(1)} %get-tuple-element.22.error_ref, ...), custom_call_target="tpu_custom_call", output_to_operand_aliasing={{0}: (4, {}), {1}: (5, {})} | custom-call | tf_op jit(solution)/shard_map/updates_tail/pallas_call | solution.py:164
  11.0 0.0 collective-permute-done.x_ref
  11.0 22.5 %all_to_all.30.parts_ref = f32[64,8,128]{2,1,0:T(8,128)S(1)} all-to-all(f32[64,8,128]{2,1,0:T(8,128)S(1)} %add.2), channel_id=1, replica_groups=mesh['dp'=16,'x'=4,'core'=2] {'dp','x'}, dimensions={0} | all-to-all | bytes 524288 | tf_op jit(solution)/shard_map/all_to_all | solution.py:330
  33.6 0.1 spread.2
  33.6 15.3 %all_to_all.31.tiles_ref = f32[64,8,128]{2,1,0:T(8,128)S(1)} all-to-all(f32[64,8,128]{2,1,0:T(8,128)S(1)} %spread.2), channel_id=1, replica_groups=mesh['dp'=16,'x'=4,'core'=2] {'dp','x'}, dimensions={0} | all-to-all | bytes 524288 | tf_op jit(solution)/shard_map/all_to_all | solution.py:339
  48.9 0.0 collective-permute-start.1
  48.9 1.3 %right_own.2 = (f32[8,128]{1,0:T(8,128)S(1)}, f32[8,8]{1,0:T(8,128)S(1)}) custom-call(f32[64,8,128]{2,1,0:T(8,128)S(1)} %all_to_all.31.tiles_ref, bf16[256,8192]{1,0:T(8,128)(2,1)S(1)} %get-tuple-element.28.high_ref, bf16[256,8192]{1,0:T(8,128)(2,1)S(1)} %get-tuple-element.29.low_ref), custom_call_target="tpu_custom_call" | custom-call | tf_op jit(solution)/shard_map/right_own/pallas_call | solution.py:235
  50.2 0.2 collective-permute-done.1.tiles_ref
  50.4 1.2 %right_both.2 = f32[16,2,8,128]{3,2,1,0:T(8,128)S(1)} custom-call(f32[8,128]{1,0:T(8,128)S(1)} %get-tuple-element.30.mine_ref, f32[64,8,128]{2,1,0:T(8,128)S(1)} %collective-permute-done.1.tiles_ref, bf16[256,8192]{1,0:T(8,128)(2,1)S(1)} %get-tuple-element.28.high_ref, bf16[256,8192]{1,0:T(8,128)(2,1)S(1)} %get-tuple-element.29.low_ref), custom_call_target="tpu_custom_call" | custom-call | tf_op jit(solution)/shard_map/right_both/pallas_call | solution.py:244
  51.7 10.9 %all_to_all.32.parts_ref = f32[16,2,8,128]{3,2,1,0:T(8,128)S(1)} all-to-all(f32[16,2,8,128]{3,2,1,0:T(8,128)S(1)} %right_both.2), channel_id=1, replica_groups=mesh['dp'=16,'x'=4,'core'=2] {'dp'}, dimensions={0} | all-to-all | bytes 262144 | tf_op jit(solution)/shard_map/all_to_all | solution.py:405
  62.6 0.7 left_other.1
  63.2 0.1 collective-permute-start.2
  63.3 0.9 left_own.1
  64.2 0.6 collective-permute-done.2.x_ref
  64.9 15.9 %all_to_all.33.parts_ref = f32[64,8,128]{2,1,0:T(8,128)S(1)} all-to-all(f32[64,8,128]{2,1,0:T(8,128)S(1)} %add.3), channel_id=1, replica_groups=mesh['dp'=16,'x'=4,'core'=2] {'dp','x'}, dimensions={0} | all-to-all | bytes 524288 | tf_op jit(solution)/shard_map/all_to_all | solution.py:330
  80.8 0.2 spread.3
  81.0 15.3 %all_to_all.34.tiles_ref.mine_ref = f32[64,8,128]{2,1,0:T(8,128)S(1)} all-to-all(f32[64,8,128]{2,1,0:T(8,128)S(1)} %spread.3), channel_id=1, replica_groups=mesh['dp'=16,'x'=4,'core'=2] {'dp','x'}, dimensions={0} | all-to-all | bytes 524288 | tf_op jit(solution)/shard_map/all_to_all | solution.py:339
  96.2 0.0 collective-permute-start.3
  96.3 1.6 %right_own.3 = (f32[8,128]{1,0:T(8,128)S(1)}, f32[8,8]{1,0:T(8,128)S(1)}) custom-call(f32[64,8,128]{2,1,0:T(8,128)S(1)} %all_to_all.34.tiles_ref.mine_ref, bf16[256,8192]{1,0:T(8,128)(2,1)S(1)} %get-tuple-element.28.high_ref, bf16[256,8192]{1,0:T(8,128)(2,1)S(1)} %get-tuple-element.29.low_ref), custom_call_target="tpu_custom_call" | custom-call | tf_op jit(solution)/shard_map/right_own/pallas_call | solution.py:235
  97.8 0.0 collective-permute-done.3.tiles_ref.other_ref
  97.9 1.6 %right_both.3 = (f32[16,2,8,128]{3,2,1,0:T(8,128)S(1)}, f32[8,8]{1,0:T(8,128)S(1)}) custom-call(f32[8,128]{1,0:T(8,128)S(1)} %get-tuple-element.34.mine_ref, f32[64,8,128]{2,1,0:T(8,128)S(1)} %collective-permute-done.3.tiles_ref.other_ref, bf16[256,8192]{1,0:T(8,128)(2,1)S(1)} %get-tuple-element.28.high_ref, bf16[256,8192]{1,0:T(8,128)(2,1)S(1)} %get-tuple-element.29.low_ref), custom_call_target="tpu_custom_call" | custom-call | tf_op jit(solution)/shard_map/right_both/pallas_call | solution.py:244
  99.5 11.0 %all_to_all.35.parts_ref = f32[16,2,8,128]{3,2,1,0:T(8,128)S(1)} all-to-all(f32[16,2,8,128]{3,2,1,0:T(8,128)S(1)} %get-tuple-element.35), channel_id=1, replica_groups=mesh['dp'=16,'x'=4,'core'=2] {'dp'}, dimensions={0} | all-to-all | bytes 262144 | tf_op jit(solution)/shard_map/all_to_all | solution.py:407
  110.5 3.5 %final.1 = (bf16[2,512,128]{2,1,0:T(8,128)(2,1)}, bf16[2,1,8192,128]{3,2,1,0:T(8,128)(2,1)}) custom-call(f32[16,2,8,128]{3,2,1,0:T(8,128)S(1)} %all_to_all.35.parts_ref, f32[64,8,128]{2,1,0:T(8,128)S(1)} %all_to_all.34.tiles_ref.mine_ref, f32[64,8,128]{2,1,0:T(8,128)S(1)} %collective-permute-done.3.tiles_ref.other_ref, ...), custom_call_target="tpu_custom_call" | custom-call | tf_op jit(solution)/shard_map/final/pallas_call | solution.py:383
  (2 shorter events, 0.1 us)
Async XLA Ops:
  9.4 1.6 %collective-permute-start = (f32[64,8,128]{2,1,0:T(8,128)S(1)}, f32[64,8,128]{2,1,0:T(8,128)S(1)}, u32[]{:S(2)}, u32[]{:S(2)}) collective-permute-start(f32[64,8,128]{2,1,0:T(8,128)S(1)} %get-tuple-element.20), channel_id=1, source_target_pairs={{0,1},{1,0},{2,3},{3,2},{4,5},{5,4},{6,7},{7,6},{8,9},{9,8},{10,11... | collective-permute-start | bytes 786440 | tf_op jit(solution)/shard_map/ppermute | solution.py:60
  48.9 1.5 %collective-permute-start.1 = (f32[64,8,128]{2,1,0:T(8,128)S(1)}, f32[64,8,128]{2,1,0:T(8,128)S(1)}, u32[]{:S(2)}, u32[]{:S(2)}) collective-permute-start(f32[64,8,128]{2,1,0:T(8,128)S(1)} %all_to_all.31.tiles_ref), channel_id=1, source_target_pairs={{0,1},{1,0},{2,3},{3,2},{4,5},{5,4},{6,7},{7,6},{8,9},{9,8},{10,11... | collective-permute-start | bytes 786440 | tf_op jit(solution)/shard_map/ppermute | solution.py:60
  63.2 1.6 %collective-permute-start.2 = (f32[64,8,128]{2,1,0:T(8,128)S(1)}, f32[64,8,128]{2,1,0:T(8,128)S(1)}, u32[]{:S(2)}, u32[]{:S(2)}) collective-permute-start(f32[64,8,128]{2,1,0:T(8,128)S(1)} %left_other.1), channel_id=1, source_target_pairs={{0,1},{1,0},{2,3},{3,2},{4,5},{5,4},{6,7},{7,6},{8,9},{9,8},{10,11... | collective-permute-start | bytes 786440 | tf_op jit(solution)/shard_map/ppermute | solution.py:60
  96.2 1.6 %collective-permute-start.3 = (f32[64,8,128]{2,1,0:T(8,128)S(1)}, f32[64,8,128]{2,1,0:T(8,128)S(1)}, u32[]{:S(2)}, u32[]{:S(2)}) collective-permute-start(f32[64,8,128]{2,1,0:T(8,128)S(1)} %all_to_all.34.tiles_ref.mine_ref), channel_id=1, source_target_pairs={{0,1},{1,0},{2,3},{3,2},{4,5},{5,4},{6,7},{7,6},{8,9},{9,8},{10,11... | collective-permute-start | bytes 786440 | tf_op jit(solution)/shard_map/ppermute | solution.py:60
